TPU v7x, 32 devices: a whole 2x2x4 slice. The times are simulated.
32 devices in a mesh: dp: 8 (over z, y), section: 2 (over core), tensor: 2 (over x).
Axes of the slice: x: 2, y: 2, z: 4, core: 2. Of those that a mesh axis runs over, the one named last changes fastest.
Arguments:
- edges_in: bfloat16 [2, 2, 2, 4096, 768], P('section', None, None, ('dp', 'tensor')), may hold values from -6 to 6
- joint_weight: bfloat16 [2, 2, 3, 768, 768], P('section', None, None, None, 'tensor'), may hold values from -0.21875 to 0.21875
- output_weight: bfloat16 [2, 2, 768, 768], P('section', None, 'tensor'), may hold values from -0.625 to 0.625
- lift_weight: bfloat16 [2, 2, 768, 3072], P('section', None, None, 'tensor'), may hold values from -0.21875 to 0.21875
- lift_bias: bfloat16 [2, 2, 3072], P('section', None, 'tensor'), may hold values from -3 to 3
- drop_weight: bfloat16 [2, 2, 3072, 768], P('section', None, 'tensor'), may hold values from -0.15625 to 0.15625
- norm_gains: bfloat16 [2, 2, 2, 768], P('section'), may hold values from 0.25 to 1.75
- norm_shifts: bfloat16 [2, 2, 2, 768], P('section'), may hold values from -2 to 2
- branch_biases: bfloat16 [2, 2, 2, 768], P('section'), may hold values from -2 to 2
- item_lengths: int32 [8, 2, 3], P('dp'), may hold values from 0 to 400, as said below
- key_keep: int32 [8, 2, 512], P('dp'), may hold values 0 or 1
Outputs:
- edges_out: bfloat16 [2, 2, 2, 4096, 768], P('section', None, None, ('dp', 'tensor'))
- grad_joint: float32 [2, 2, 3, 768, 768], P('section', None, None, None, 'tensor')
- grad_output: float32 [2, 2, 768, 768], P('section', None, 'tensor')
- grad_lift: float32 [2, 2, 768, 3072], P('section', None, None, 'tensor')
- grad_lift_bias: float32 [2, 2, 3072], P('section', None, 'tensor')
- grad_drop: float32 [2, 2, 3072, 768], P('section', None, 'tensor')
- grad_gains: float32 [2, 2, 2, 768], P('section')
- grad_shifts: float32 [2, 2, 2, 768], P('section')
- grad_biases: float32 [2, 2, 2, 768], P('section')
Inputs may be any that keep to these rules, and one draw needn't show every extreme that they name: `item_lengths`: each entry is 0, 144, 225 or 400; within a pack the nonzero entries come first and sum to at most 512.
All inputs are finite; a program needn't handle non-finite values. No bound on the sum of `key_keep` on one device may be relied on, other than what follows from the above.
Results may differ from a plain program's by a relative error of at most 0.02.
Values may be sent and summed in bfloat16 or wider, within the bound.
A program may use at most 320 MiB of HBM per device.

v0:
```python
from functools import partial

import jax
import jax.numpy as jnp
from jax import lax
from jax.sharding import PartitionSpec as P

HEADS = 12
HEAD_DIM = 64


EPSILON = 1e-06


def from_behind(value, axis, steps):
    count = lax.axis_size(axis)
    initial, last = (max(0, -steps), min(count, count - steps))
    return lax.ppermute(value, axis, [(source, source + steps) for source in range(initial, last)])


def geometry(lengths, keep_row):
    rows_all = keep_row.shape[0]
    slots = lengths.shape[0]
    positions = jnp.arange(rows_all, dtype=jnp.int32)
    item_ends = jnp.cumsum(lengths)
    segment = jnp.sum((positions[:, None] >= item_ends[None, :]).astype(jnp.int32), axis=1)
    following = jnp.arange(1, slots + 1, dtype=jnp.int32)
    item_ids = jnp.arange(slots, dtype=jnp.int32)
    begin = jnp.sum(
        jnp.where(segment[:, None] == following[None, :], item_ends[None, :], 0), axis=1
    )
    length = jnp.sum(jnp.where(segment[:, None] == item_ids[None, :], lengths[None, :], 0), axis=1)
    grid_side = jnp.where(length == 144, 12, jnp.where(length == 225, 15, 20)).astype(jnp.int32)
    offset = positions - begin
    grid_row = (offset // grid_side).astype(jnp.float32)
    column = (offset % grid_side).astype(jnp.float32)
    row_gap = grid_row[:, None] - grid_row[None, :]
    col_gap = column[:, None] - column[None, :]
    distance = jnp.sqrt(row_gap * row_gap + col_gap * col_gap)
    allowed = (segment[:, None] == segment[None, :]) & (
        (keep_row[None, :] == 1) | (positions[:, None] == positions[None, :])
    )
    return (allowed, distance)


def normalize(values_in, gain_vec, shift_vec):
    row_mean = jnp.mean(values_in, axis=-1, keepdims=True)
    centred = values_in - row_mean
    variance = jnp.mean(centred * centred, axis=-1, keepdims=True)
    return centred * lax.rsqrt(variance + EPSILON) * gain_vec + shift_vec


def select_batch(stacked, batch_index):
    return lax.dynamic_index_in_dim(stacked, batch_index, 1, keepdims=False)


def place_batch(stacked, piece, batch_index):
    return lax.dynamic_update_index_in_dim(stacked, piece, batch_index, 1)


def layer_forward(inputs, weights, is_cross, allowed, distance, slopes):
    (
        joint_weight,
        output_weight,
        lift_weight,
        lift_bias,
        drop_weight,
        norm_gains,
        norm_shifts,
        branch_biases,
    ) = weights
    input_f32 = inputs.astype(jnp.float32)
    gains_all = norm_gains.astype(jnp.float32)
    shifts_all = norm_shifts.astype(jnp.float32)
    biases_all = branch_biases.astype(jnp.float32)
    normed = normalize(input_f32, gains_all[:, 0][:, None, :], shifts_all[:, 0][:, None, :]).astype(
        jnp.bfloat16
    )
    normed_all = lax.all_gather(normed, "tensor", axis=1, tiled=True)
    source = jnp.where(is_cross, jnp.stack([normed_all[0], normed_all[0]]), normed_all)
    rows_all = normed_all.shape[1]
    query_scale = HEAD_DIM ** (-0.5)
    queries = (
        query_scale
        * jnp.einsum(
            "bnd,bde->bne", normed_all, joint_weight[:, 0], preferred_element_type=jnp.float32
        )
    ).astype(jnp.bfloat16)
    keys_low = jnp.einsum(
        "bnd,bde->bne", source, joint_weight[:, 1], preferred_element_type=jnp.float32
    ).astype(jnp.bfloat16)
    values_low = jnp.einsum(
        "bnd,bde->bne", source, joint_weight[:, 2], preferred_element_type=jnp.float32
    ).astype(jnp.bfloat16)
    local_heads = queries.shape[2] // HEAD_DIM
    query_heads = queries.reshape(2, rows_all, local_heads, HEAD_DIM)
    key_heads = keys_low.reshape(2, rows_all, local_heads, HEAD_DIM)
    value_heads = values_low.reshape(2, rows_all, local_heads, HEAD_DIM)
    scores = jnp.einsum(
        "bqhe,bkhe->bhqk", query_heads, key_heads, preferred_element_type=jnp.float32
    )
    scores = scores - slopes[None, :, None, None] * distance[None, None]
    scores = jnp.where(allowed[None, None], scores, -1000000000.0)
    shifted = scores - jnp.max(scores, axis=-1, keepdims=True)
    expo = jnp.exp(shifted)
    softmax_probs = expo / jnp.sum(expo, axis=-1, keepdims=True)
    probs_low = softmax_probs.astype(jnp.bfloat16)
    context = jnp.einsum(
        "bhqk,bkhe->bqhe", probs_low, value_heads, preferred_element_type=jnp.float32
    )
    context = context.reshape(2, rows_all, local_heads * HEAD_DIM).astype(jnp.bfloat16)
    attn_terms = jnp.einsum(
        "bnh,bhd->bnd", context, output_weight, preferred_element_type=jnp.float32
    )
    attended = (
        lax.psum_scatter(
            attn_terms.astype(jnp.bfloat16), "tensor", scatter_dimension=1, tiled=True
        ).astype(jnp.float32)
        + biases_all[:, 0][:, None, :]
    )
    middle = input_f32 + attended
    mixed_low = normalize(middle, gains_all[:, 1][:, None, :], shifts_all[:, 1][:, None, :]).astype(
        jnp.bfloat16
    )
    mixed_all = lax.all_gather(mixed_low, "tensor", axis=1, tiled=True)
    hidden = (
        jnp.einsum("bnd,bdf->bnf", mixed_all, lift_weight, preferred_element_type=jnp.float32)
        + lift_bias.astype(jnp.float32)[:, None, :]
    )
    active = jax.nn.gelu(hidden, approximate=False).astype(jnp.bfloat16)
    mlp_terms = jnp.einsum("bnf,bfd->bnd", active, drop_weight, preferred_element_type=jnp.float32)
    result = (
        middle
        + lax.psum_scatter(
            mlp_terms.astype(jnp.bfloat16), "tensor", scatter_dimension=1, tiled=True
        ).astype(jnp.float32)
        + biases_all[:, 1][:, None, :]
    )
    stored = (
        normed_all,
        source,
        query_heads,
        key_heads,
        value_heads,
        softmax_probs,
        probs_low,
        context,
        middle,
        mixed_all,
        hidden,
        active,
    )
    return (result, stored)


def layer_backward(inputs, grad_rows, weights, is_cross, allowed, distance, slopes):
    (
        joint_weight,
        output_weight,
        lift_weight,
        lift_bias,
        drop_weight,
        norm_gains,
        norm_shifts,
        branch_biases,
    ) = weights
    result, stored = layer_forward(inputs, weights, is_cross, allowed, distance, slopes)
    (
        normed_all,
        source,
        query_heads,
        key_heads,
        value_heads,
        softmax_probs,
        probs_low,
        context,
        middle,
        mixed_all,
        hidden,
        active,
    ) = stored
    gains_all = norm_gains.astype(jnp.float32)
    shifts_all = norm_shifts.astype(jnp.float32)
    rows_all = normed_all.shape[1]
    local_heads = query_heads.shape[2]
    query_scale = HEAD_DIM ** (-0.5)
    grad_all = lax.all_gather(grad_rows, "tensor", axis=1, tiled=True)
    grad_drop = jnp.einsum("bnf,bnd->bfd", active, grad_all, preferred_element_type=jnp.float32)
    grad_active = jnp.einsum(
        "bnd,bfd->bnf", grad_all, drop_weight, preferred_element_type=jnp.float32
    )
    gelu_value, gelu_pull = jax.vjp(partial(jax.nn.gelu, approximate=False), hidden)
    grad_hidden = gelu_pull(grad_active)[0].astype(jnp.bfloat16)
    grad_lift_bias = jnp.sum(grad_hidden.astype(jnp.float32), axis=1)
    grad_lift = jnp.einsum(
        "bnd,bnf->bdf", mixed_all, grad_hidden, preferred_element_type=jnp.float32
    )
    mixed_terms = jnp.einsum(
        "bnf,bdf->bnd", grad_hidden, lift_weight, preferred_element_type=jnp.float32
    )
    grad_mixed = lax.psum_scatter(
        mixed_terms.astype(jnp.bfloat16), "tensor", scatter_dimension=1, tiled=True
    ).astype(jnp.float32)
    grad_out_f32 = grad_rows.astype(jnp.float32)
    second_value, second_pull = jax.vjp(
        normalize, middle, gains_all[:, 1][:, None, :], shifts_all[:, 1][:, None, :]
    )
    grad_mid_norm, grad_gain_two, grad_shift_two = second_pull(grad_mixed)
    grad_middle = grad_out_f32 + grad_mid_norm
    grad_attn_low = grad_middle.astype(jnp.bfloat16)
    grad_bias_attn = jnp.sum(grad_attn_low.astype(jnp.float32), axis=1)
    grad_bias_mlp = jnp.sum(grad_out_f32, axis=1)
    grad_attn_all = lax.all_gather(grad_attn_low, "tensor", axis=1, tiled=True)
    grad_output = jnp.einsum(
        "bnh,bnd->bhd", context, grad_attn_all, preferred_element_type=jnp.float32
    )
    grad_context = jnp.einsum(
        "bnd,bhd->bnh", grad_attn_all, output_weight, preferred_element_type=jnp.float32
    ).astype(jnp.bfloat16)
    grad_context = grad_context.reshape(2, rows_all, local_heads, HEAD_DIM)
    grad_probs = jnp.einsum(
        "bqhe,bkhe->bhqk", grad_context, value_heads, preferred_element_type=jnp.float32
    )
    grad_scores = (
        softmax_probs * (grad_probs - jnp.sum(grad_probs * softmax_probs, axis=-1, keepdims=True))
    ).astype(jnp.bfloat16)
    grad_values = jnp.einsum(
        "bhqk,bqhe->bkhe", probs_low, grad_context, preferred_element_type=jnp.float32
    ).astype(jnp.bfloat16)
    grad_keys = jnp.einsum(
        "bhqk,bqhe->bkhe", grad_scores, query_heads, preferred_element_type=jnp.float32
    ).astype(jnp.bfloat16)
    grad_queries = (
        query_scale
        * jnp.einsum("bhqk,bkhe->bqhe", grad_scores, key_heads, preferred_element_type=jnp.float32)
    ).astype(jnp.bfloat16)
    grad_queries = grad_queries.reshape(2, rows_all, local_heads * HEAD_DIM)
    grad_keys = grad_keys.reshape(2, rows_all, local_heads * HEAD_DIM)
    grad_values = grad_values.reshape(2, rows_all, local_heads * HEAD_DIM)
    grad_joint = jnp.stack(
        [
            jnp.einsum(
                "bnd,bne->bde", normed_all, grad_queries, preferred_element_type=jnp.float32
            ),
            jnp.einsum("bnd,bne->bde", source, grad_keys, preferred_element_type=jnp.float32),
            jnp.einsum("bnd,bne->bde", source, grad_values, preferred_element_type=jnp.float32),
        ],
        axis=1,
    )
    own_part = jnp.einsum(
        "bne,bde->bnd", grad_queries, joint_weight[:, 0], preferred_element_type=jnp.float32
    )
    far_part = jnp.einsum(
        "bne,bde->bnd", grad_keys, joint_weight[:, 1], preferred_element_type=jnp.float32
    )
    far_part = far_part + jnp.einsum(
        "bne,bde->bnd", grad_values, joint_weight[:, 2], preferred_element_type=jnp.float32
    )
    cross_part = jnp.stack([far_part[0] + far_part[1], jnp.zeros_like(far_part[1])])
    normed_terms = own_part + jnp.where(is_cross, cross_part, far_part)
    grad_normed = lax.psum_scatter(
        normed_terms.astype(jnp.bfloat16), "tensor", scatter_dimension=1, tiled=True
    ).astype(jnp.float32)
    first_value, first_pull = jax.vjp(
        normalize,
        inputs.astype(jnp.float32),
        gains_all[:, 0][:, None, :],
        shifts_all[:, 0][:, None, :],
    )
    grad_in_norm, grad_gain_one, grad_shift_one = first_pull(grad_normed)
    grad_inputs = grad_middle + grad_in_norm
    grad_gains = jnp.stack([grad_gain_one[:, 0], grad_gain_two[:, 0]], axis=1)
    grad_shifts = jnp.stack([grad_shift_one[:, 0], grad_shift_two[:, 0]], axis=1)
    grad_biases = jnp.stack([grad_bias_attn, grad_bias_mlp], axis=1)
    return (
        grad_inputs,
        (
            grad_joint,
            grad_output,
            grad_lift,
            grad_lift_bias,
            grad_drop,
            grad_gains,
            grad_shifts,
            grad_biases,
        ),
    )


def local(
    edges_in,
    joint_weight,
    output_weight,
    lift_weight,
    lift_bias,
    drop_weight,
    norm_gains,
    norm_shifts,
    branch_biases,
    item_lengths,
    key_keep,
):
    weights = tuple(
        (
            arr[0]
            for arr in (
                joint_weight,
                output_weight,
                lift_weight,
                lift_bias,
                drop_weight,
                norm_gains,
                norm_shifts,
                branch_biases,
            )
        )
    )
    section_index = lax.axis_index("section")
    is_first = section_index == 0
    is_cross = jnp.logical_not(is_first)
    held_rows = edges_in[0]
    batches = held_rows.shape[1]
    heads_here = joint_weight.shape[-1] // HEAD_DIM
    head_ids = (
        lax.axis_index("tensor") * heads_here + jnp.arange(heads_here, dtype=jnp.int32)
    ).astype(jnp.float32)
    slopes = jnp.power(2.0, -8.0 * (head_ids + 1.0) / HEADS)
    lengths_here = item_lengths[0]
    keeps_here = key_keep[0]
    stash = jnp.zeros_like(held_rows)
    joined_out = jnp.zeros_like(held_rows)
    arrived = jnp.zeros_like(held_rows[:, 0])
    for moment in range(batches + 1):
        number = moment - section_index
        is_valid = (number >= 0) & (number < batches)
        batch_index = jnp.clip(number, 0, batches - 1)
        block_in = jnp.where(is_first, select_batch(held_rows, batch_index), arrived)
        allowed, distance = geometry(
            lax.dynamic_index_in_dim(lengths_here, batch_index, 0, keepdims=False),
            lax.dynamic_index_in_dim(keeps_here, batch_index, 0, keepdims=False),
        )
        stash = jnp.where(is_valid, place_batch(stash, block_in, batch_index), stash)
        result, stored = layer_forward(block_in, weights, is_cross, allowed, distance, slopes)
        result_low = result.astype(jnp.bfloat16)
        joined_out = jnp.where(
            is_valid, place_batch(joined_out, result_low, batch_index), joined_out
        )
        if moment < batches:
            arrived = from_behind(result_low, "section", 1)
    input_grads = jnp.zeros_like(held_rows)
    returned = jnp.zeros_like(held_rows[:, 0])
    totals = None
    for moment in range(batches + 1):
        number = batches - moment - section_index
        is_valid = (number >= 0) & (number < batches)
        batch_index = jnp.clip(number, 0, batches - 1)
        grad_rows = jnp.where(is_first, returned, select_batch(held_rows, batch_index))
        block_in = select_batch(stash, batch_index)
        allowed, distance = geometry(
            lax.dynamic_index_in_dim(lengths_here, batch_index, 0, keepdims=False),
            lax.dynamic_index_in_dim(keeps_here, batch_index, 0, keepdims=False),
        )
        grad_inputs, grads = layer_backward(
            block_in, grad_rows, weights, is_cross, allowed, distance, slopes
        )
        grad_low = grad_inputs.astype(jnp.bfloat16)
        input_grads = jnp.where(
            is_valid, place_batch(input_grads, grad_low, batch_index), input_grads
        )
        valid_weight = is_valid.astype(jnp.float32)
        grads = tuple((valid_weight * piece for piece in grads))
        if totals is None:
            totals = tuple(grads)
        else:
            totals = tuple((former + latter for former, latter in zip(totals, grads)))
        if moment < batches:
            returned = from_behind(grad_low, "section", -1)
    summed = (
        lax.psum(totals[0].astype(jnp.bfloat16), "dp").astype(jnp.float32),
        lax.psum(totals[1].astype(jnp.bfloat16), "dp").astype(jnp.float32),
        lax.psum(totals[2].astype(jnp.bfloat16), "dp").astype(jnp.float32),
        lax.psum(totals[3].astype(jnp.bfloat16), "dp").astype(jnp.float32),
        lax.psum(totals[4].astype(jnp.bfloat16), "dp").astype(jnp.float32),
        lax.psum(totals[5].astype(jnp.bfloat16), "dp").astype(jnp.float32),
        lax.psum(totals[6].astype(jnp.bfloat16), "dp").astype(jnp.float32),
        lax.psum(totals[7].astype(jnp.bfloat16), "dp").astype(jnp.float32),
    )
    small_sums = (
        lax.psum(summed[5].astype(jnp.bfloat16), "tensor").astype(jnp.float32),
        lax.psum(summed[6].astype(jnp.bfloat16), "tensor").astype(jnp.float32),
        lax.psum(summed[7].astype(jnp.bfloat16), "tensor").astype(jnp.float32),
    )
    edges_out = jnp.where(is_first, input_grads, joined_out)[None]
    return (
        edges_out,
        summed[0][None],
        summed[1][None],
        summed[2][None],
        summed[3][None],
        summed[4][None],
        small_sums[0][None],
        small_sums[1][None],
        small_sums[2][None],
    )


def solution(mesh):
    in_specs = (
        P("section", None, None, ("dp", "tensor"), None),
        P("section", None, None, None, "tensor"),
        P("section", None, "tensor", None),
        P("section", None, None, "tensor"),
        P("section", None, "tensor"),
        P("section", None, "tensor", None),
        P("section", None, None, None),
        P("section", None, None, None),
        P("section", None, None, None),
        P("dp", None, None),
        P("dp", None, None),
    )
    out_specs = (
        P("section", None, None, ("dp", "tensor"), None),
        P("section", None, None, None, "tensor"),
        P("section", None, "tensor", None),
        P("section", None, None, "tensor"),
        P("section", None, "tensor"),
        P("section", None, "tensor", None),
        P("section", None, None, None),
        P("section", None, None, None),
        P("section", None, None, None),
    )
    return jax.shard_map(local, mesh=mesh, in_specs=in_specs, out_specs=out_specs, check_vma=False)
```

profile of v0, /device:TPU:0, one launch (start us, length us, event | category | flops | bytes accessed | tf_op | source)
XLA Modules:
  0.0 1783.0 jit_solution(6218019224953346239)
XLA Ops:
  17.3 6.3 copy.88
  25.1 7.6 broadcast_multiply_fusion
  32.7 12.1 all-gather.19.cloned.1.call-done
  51.7 12.4 fusion.574
  76.0 25.0 %reduce-scatter.16.cloned.1.call-done = bf16[2,256,768]{2,1,0:T(8,128)(2,1)} async-done(((bf16[2,512,768]{2,1,0:T(8,128)(2,1)}), bf16[2,256,768]{2,1,0:T(8,128)(2,1)}) %reduce-scatter.16.cloned.1.call-update) | async-done | bytes 786448 | tf_op jit(solution)/shard_map/reduce_scatter | solution.py:116
  108.0 25.4 %all-gather.21.cloned.1.call-done = bf16[2,512,768]{2,1,0:T(8,128)(2,1)} async-done(((bf16[2,256,768]{2,1,0:T(8,128)(2,1)}), bf16[2,512,768]{2,1,0:T(8,128)(2,1)}) %all-gather.21.cloned.1.call-update) | async-done | bytes 1572880 | tf_op jit(solution)/shard_map/all_gather | solution.py:125
  133.4 7.6 fusion.335
  141.0 19.5 %fusion.272 = bf16[2,512,768]{2,1,0:T(8,128)(2,1)} fusion(bf16[1,2,1536,768]{3,2,1,0:T(8,128)(2,1)} %param.16, f32[2,512,1536]{2,1,0:T(8,128)S(1)} %get-tuple-element.159, f32[2,1536]{1,0:T(2,128)S(1)} %copy-done.110, u8[512,1536]{1,0:T(8,128)(4,1)S(1)} %get-tuple-element.38, u8[512,1536]{1,0:T(8,128)(4,1)S(1)} %get-tuple-element.37), kind=kOutput, calls=%fused_computation.429 | convolution fusion | flops 2528378880 | bytes 14168064 | tf_op jit(solution)/shard_map/bnf,bfd->bnd/dot_general | solution.py:131
  162.0 24.7 %reduce-scatter.18.cloned.1.call-done = bf16[2,256,768]{2,1,0:T(8,128)(2,1)} async-done(((bf16[2,512,768]{2,1,0:T(8,128)(2,1)}), bf16[2,256,768]{2,1,0:T(8,128)(2,1)}) %reduce-scatter.18.cloned.1.call-update) | async-done | bytes 786448 | tf_op jit(solution)/shard_map/reduce_scatter | solution.py:134
  195.3 26.3 %all-gather.23.cloned.1.call-done = bf16[2,512,768]{2,1,0:T(8,128)(2,1)} async-done(((bf16[2,256,768]{2,1,0:T(8,128)(2,1)}), bf16[2,512,768]{2,1,0:T(8,128)(2,1)}) %all-gather.23.cloned.1.call-update) | async-done | bytes 1572880 | tf_op jit(solution)/shard_map/all_gather | solution.py:79
  229.4 12.6 fusion.575
  252.6 26.2 %reduce-scatter.20.cloned.1.call-done = bf16[2,256,768]{2,1,0:T(8,128)(2,1)} async-done(((bf16[2,512,768]{2,1,0:T(8,128)(2,1)}), bf16[2,256,768]{2,1,0:T(8,128)(2,1)}) %reduce-scatter.20.cloned.1.call-update) | async-done | bytes 786448 | tf_op jit(solution)/shard_map/reduce_scatter | solution.py:116
  283.6 27.1 %all-gather.25.cloned.1.call-done = bf16[2,512,768]{2,1,0:T(8,128)(2,1)} async-done(((bf16[2,256,768]{2,1,0:T(8,128)(2,1)}), bf16[2,512,768]{2,1,0:T(8,128)(2,1)}) %all-gather.25.cloned.1.call-update) | async-done | bytes 1572880 | tf_op jit(solution)/shard_map/all_gather | solution.py:125
  310.7 7.2 fusion.336
  317.9 19.5 %fusion.277 = bf16[2,512,768]{2,1,0:T(8,128)(2,1)} fusion(bf16[1,2,1536,768]{3,2,1,0:T(8,128)(2,1)} %param.16, f32[2,512,1536]{2,1,0:T(8,128)S(1)} %get-tuple-element.162, f32[2,1536]{1,0:T(2,128)S(1)} %copy-done.111, u8[512,1536]{1,0:T(8,128)(4,1)S(1)} %get-tuple-element.36, u8[512,1536]{1,0:T(8,128)(4,1)S(1)} %get-tuple-element.35), kind=kOutput, calls=%fused_computation.430 | convolution fusion | flops 2528378880 | bytes 14168064 | tf_op jit(solution)/shard_map/bnf,bfd->bnd/dot_general | solution.py:131
  339.3 24.3 %reduce-scatter.22.cloned.1.call-done = bf16[2,256,768]{2,1,0:T(8,128)(2,1)} async-done(((bf16[2,512,768]{2,1,0:T(8,128)(2,1)}), bf16[2,256,768]{2,1,0:T(8,128)(2,1)}) %reduce-scatter.22.cloned.1.call-update) | async-done | bytes 786448 | tf_op jit(solution)/shard_map/reduce_scatter | solution.py:134
  379.0 25.8 %all-gather.27.cloned.1.call-done = bf16[2,512,768]{2,1,0:T(8,128)(2,1)} async-done(((bf16[2,256,768]{2,1,0:T(8,128)(2,1)}), bf16[2,512,768]{2,1,0:T(8,128)(2,1)}) %all-gather.27.cloned.1.call-update) | async-done | bytes 1572880 | tf_op jit(solution)/shard_map/all_gather | solution.py:79
  411.8 13.3 fusion.576
  442.3 21.3 %reduce-scatter.24.cloned.1.call-done = bf16[2,256,768]{2,1,0:T(8,128)(2,1)} async-done(((bf16[2,512,768]{2,1,0:T(8,128)(2,1)}), bf16[2,256,768]{2,1,0:T(8,128)(2,1)}) %reduce-scatter.24.cloned.1.call-update) | async-done | bytes 786448 | tf_op jit(solution)/shard_map/reduce_scatter | solution.py:116
  474.0 24.8 %all-gather.29.cloned.1.call-done = bf16[2,512,768]{2,1,0:T(8,128)(2,1)} async-done(((bf16[2,256,768]{2,1,0:T(8,128)(2,1)}), bf16[2,512,768]{2,1,0:T(8,128)(2,1)}) %all-gather.29.cloned.1.call-update) | async-done | bytes 1572880 | tf_op jit(solution)/shard_map/all_gather | solution.py:125
  498.9 7.6 fusion.337
  509.1 14.9 fusion.21
  527.6 11.4 convert_reduce_fusion.2
  540.7 6.1 fusion.287
  547.1 9.3 all-gather.51.cloned.1.call-done
  564.7 13.7 fusion.577
  595.5 13.2 fusion.578
  626.4 13.3 fusion.579
  648.9 22.6 %reduce-scatter.42.cloned.1.call-done = bf16[2,256,768]{2,1,0:T(8,128)(2,1)} async-done(((bf16[2,512,768]{2,1,0:T(8,128)(2,1)}), bf16[2,256,768]{2,1,0:T(8,128)(2,1)}) %reduce-scatter.42.cloned.1.call-update) | async-done | bytes 786448 | tf_op jit(solution)/shard_map/reduce_scatter | solution.py:116
  675.8 24.6 %reduce-scatter.30.cloned.1.call-done = bf16[2,256,768]{2,1,0:T(8,128)(2,1)} async-done(((bf16[2,512,768]{2,1,0:T(8,128)(2,1)}), bf16[2,256,768]{2,1,0:T(8,128)(2,1)}) %reduce-scatter.30.cloned.1.call-update) | async-done | bytes 786448 | tf_op jit(solution)/shard_map/reduce_scatter | solution.py:116
  700.4 28.9 %reduce-scatter.36.cloned.1.call-done = bf16[2,256,768]{2,1,0:T(8,128)(2,1)} async-done(((bf16[2,512,768]{2,1,0:T(8,128)(2,1)}), bf16[2,256,768]{2,1,0:T(8,128)(2,1)}) %reduce-scatter.36.cloned.1.call-update) | async-done | bytes 786448 | tf_op jit(solution)/shard_map/reduce_scatter | solution.py:116
  737.1 26.9 %all-gather.33.cloned.1.call-done = bf16[2,512,768]{2,1,0:T(8,128)(2,1)} async-done(((bf16[2,256,768]{2,1,0:T(8,128)(2,1)}), bf16[2,512,768]{2,1,0:T(8,128)(2,1)}) %all-gather.33.cloned.1.call-update) | async-done | bytes 1572880 | tf_op jit(solution)/shard_map/all_gather | solution.py:213
  766.3 10.3 multiply_reduce_fusion.2
  776.6 6.8 fusion.345
  783.4 7.0 multiply_convert_fusion.2
  801.0 24.9 %reduce-scatter.28.cloned.1.call-done = bf16[2,256,768]{2,1,0:T(8,128)(2,1)} async-done(((bf16[2,512,768]{2,1,0:T(8,128)(2,1)}), bf16[2,256,768]{2,1,0:T(8,128)(2,1)}) %reduce-scatter.28.cloned.1.call-update) | async-done | bytes 786448 | tf_op jit(solution)/shard_map/reduce_scatter | solution.py:261
  845.3 16.9 all-gather.37.cloned.1.call-done
  862.2 7.6 fusion.338
  872.5 14.8 fusion.22
  891.0 11.4 convert_reduce_fusion.1
  904.1 6.1 fusion.290
  912.8 23.7 %reduce-scatter.32.cloned.1.call-done = bf16[2,256,768]{2,1,0:T(8,128)(2,1)} async-done(((bf16[2,512,768]{2,1,0:T(8,128)(2,1)}), bf16[2,256,768]{2,1,0:T(8,128)(2,1)}) %reduce-scatter.32.cloned.1.call-update) | async-done | bytes 786448 | tf_op jit(solution)/shard_map/reduce_scatter | solution.py:201
  948.3 26.9 %all-gather.41.cloned.1.call-done = bf16[2,512,768]{2,1,0:T(8,128)(2,1)} async-done(((bf16[2,256,768]{2,1,0:T(8,128)(2,1)}), bf16[2,512,768]{2,1,0:T(8,128)(2,1)}) %all-gather.41.cloned.1.call-update) | async-done | bytes 1572880 | tf_op jit(solution)/shard_map/all_gather | solution.py:213
  977.5 10.2 multiply_reduce_fusion.1
  987.8 6.8 fusion.351
  994.6 7.1 multiply_convert_fusion.1
  1012.3 24.8 %reduce-scatter.34.cloned.1.call-done = bf16[2,256,768]{2,1,0:T(8,128)(2,1)} async-done(((bf16[2,512,768]{2,1,0:T(8,128)(2,1)}), bf16[2,256,768]{2,1,0:T(8,128)(2,1)}) %reduce-scatter.34.cloned.1.call-update) | async-done | bytes 786448 | tf_op jit(solution)/shard_map/reduce_scatter | solution.py:261
  1048.8 11.0 fusion.120
  1065.8 8.1 fusion.97
  1073.9 20.7 %all-gather.53.cloned.1.call-done = bf16[2,512,768]{2,1,0:T(8,128)(2,1)} async-done(((bf16[2,256,768]{2,1,0:T(8,128)(2,1)}), bf16[2,512,768]{2,1,0:T(8,128)(2,1)}) %all-gather.53.cloned.1.call-update) | async-done | bytes 1572880 | tf_op jit(solution)/shard_map/all_gather | solution.py:125
  1094.5 14.2 fusion.340
  1108.7 14.6 all-gather.47.cloned.1.call-done
  1123.3 21.2 %convert_reduce_fusion = (f32[2,1536]{1,0:T(2,128)}, bf16[2,512,1536]{2,1,0:T(8,128)(2,1)S(1)}) fusion(u8[512,1536]{1,0:T(8,128)(4,1)} %get-tuple-element.73, u8[512,1536]{1,0:T(8,128)(4,1)} %get-tuple-element.74, bf16[2,512,768]{2,1,0:T(8,128)(2,1)} %all-gather.47.cloned.1.call-done, bf16[1,2,1536,768]{3,2,1,0:T(8,128)(2,1)} %param.16, ...), kind=kOutput, calls=%fused_computation.87 | convolution fusion | flops 2541745152 | bytes 17326080 | tf_op jit(solution)/shard_map/bnd,bfd->bnf/dot_general | solution.py:189
  1146.2 6.1 fusion.293
  1152.6 8.9 fusion.582
  1177.7 9.7 fusion.121
  1195.8 20.7 %fusion.282 = bf16[2,512,768]{2,1,0:T(8,128)(2,1)} fusion(bf16[1,2,1536,768]{3,2,1,0:T(8,128)(2,1)} %param.16, f32[2,512,1536]{2,1,0:T(8,128)} %get-tuple-element.177, f32[2,1536]{1,0:T(2,128)} %bitcast_convert_fusion, u8[512,1536]{1,0:T(8,128)(4,1)} %get-tuple-element.28, u8[512,1536]{1,0:T(8,128)(4,1)} %get-tuple-element.27), kind=kOutput, calls=%fused_computation.431 | convolution fusion | flops 2528378880 | bytes 14168064 | tf_op jit(solution)/shard_map/bnf,bfd->bnd/dot_general | solution.py:131
  1229.0 20.2 %fusion.118 = bf16[1,2,1536,768]{3,2,1,0:T(8,128)(2,1)} fusion(bf16[2,512,768]{2,1,0:T(8,128)(2,1)S(1)} %copy-done.192, f32[]{:T(128)S(6)} %convert_element_type.779, f32[2,1536,768]{2,1,0:T(8,128)} %fusion.121, f32[]{:T(128)S(6)} %convert_element_type.778, f32[2,1536,768]{2,1,0:T(8,128)S(1)} %bitcast.650, f32[]{:T(128)S(6)} %convert_element_type.777, ...), kind=kOutput, calls=%fused_computation.223 | convolution fusion | flops 2541748224 | bytes 33042444 | tf_op jit(solution)/shard_map/bnf,bnd->bfd/dot_general | solution.py:188
  1251.6 10.4 multiply_reduce_fusion
  1264.4 7.1 multiply_convert_fusion
  1286.8 13.9 fusion.117
  1346.4 39.4 %all-reduce.3 = (bf16[1,2,1536]{2,1,0:T(2,128)(2,1)S(1)}, bf16[2,2,768]{2,1,0:T(2,128)(2,1)S(1)}, bf16[2,2,768]{2,1,0:T(2,128)(2,1)S(1)}, bf16[2,2,768]{2,1,0:T(2,128)(2,1)S(1)}) all-reduce(bf16[1,2,1536]{2,1,0:T(2,128)(2,1)S(1)} %copy-done.170, ...), channel_id=1, replica_groups=mesh['dp'=8,'section'=2,'tensor'=2] {'dp'}, use_global_device_ids=true, to_apply=%region_84.85 | all-reduce | flops 12288 | bytes 49152 | tf_op jit(solution)/shard_map/psum | solution.py:382
  1386.4 7.4 all-reduce.5
  1395.6 363.6 %all-reduce.8.cloned.1.call-done = (bf16[1,2,3,768,384]{4,3,1,2,0:T(8,128)(2,1)}, bf16[1,2,384,768]{3,2,1,0:T(8,128)(2,1)}, bf16[1,2,768,1536]{3,2,1,0:T(8,128)(2,1)}, bf16[1,2,1536,768]{3,2,1,0:T(8,128)(2,1)}) async-done(((bf16[1,2,3,768,384]{4,3,1,2,0:T(8,128)(2,1)}, bf16[1,2,384,768]{3,2,1,0:T(8,128)(2,1)}, bf16[1,2,768,1536]{3,2,1,0:T(8,128)(2,1)}, bf16[1,2,1536,768]{3,2,1,0:T(8,128)(2,1)}), ...) | async-done | bytes 14155792 | tf_op jit(solution)/shard_map/psum | solution.py:379
  (751 shorter events, 401.3 us)
Async XLA Ops:
  7.2 65.3 %copy-start = (bf16[1,2,384,768]{3,2,1,0:T(8,128)(2,1)S(1)}, bf16[1,2,384,768]{3,2,1,0:T(8,128)(2,1)}, u32[]{:S(2)}) copy-start(bf16[1,2,384,768]{3,2,1,0:T(8,128)(2,1)} %param.13) | copy-start | bytes 3538948
  7.2 37.6 %all-gather.19.cloned.1.call-start = ((), (), s32[]{:S(2)}) async-start(), calls=%async_computation.15 | async-start | bytes 2359296 | tf_op jit(solution)/shard_map/all_gather | solution.py:79
  14.7 86.2 %reduce-scatter.16.cloned.1.call-start = ((), (), s32[]{:S(2)}) async-start(), calls=%async_computation.16 | async-start | bytes 2359296 | tf_op jit(solution)/shard_map/reduce_scatter | solution.py:116
  16.5 35.2 %copy-start.50 = (pred[512,512]{0,1:T(8,128)(4,1)}, pred[512,512]{0,1:T(8,128)(4,1)S(1)}, u32[]{:S(2)}) copy-start(pred[512,512]{0,1:T(8,128)(4,1)S(1)} %fusion.393) | copy-start | bytes 786436
  72.4 28.5 %copy-start.3 = (bf16[1,2,2,256,768]{4,3,2,1,0:T(8,128)(2,1)S(1)}, bf16[1,2,2,256,768]{4,3,2,1,0:T(8,128)(2,1)}, u32[]{:S(2)}) copy-start(bf16[1,2,2,256,768]{4,3,2,1,0:T(8,128)(2,1)} %param.11) | copy-start | bytes 4718596
  74.7 58.7 %all-gather.21.cloned.1.call-start = ((), (), s32[]{:S(2)}) async-start(), calls=%async_computation.17 | async-start | bytes 2359296 | tf_op jit(solution)/shard_map/all_gather | solution.py:125
  75.4 1118.0 %copy-start.52 = (f32[2,1,768]{2,0,1:T(2,128)}, f32[2,1,768]{2,0,1:T(2,128)S(1)}, u32[]{:S(2)}) copy-start(f32[2,1,768]{2,0,1:T(2,128)S(1)} %copy.231) | copy-start | bytes 18436
  76.0 1117.4 %copy-start.86 = (f32[2,768]{1,0:T(2,128)}, f32[2,768]{1,0:T(2,128)S(1)}, u32[]{:S(2)}) copy-start(f32[2,768]{1,0:T(2,128)S(1)} %get-tuple-element.192) | copy-start | bytes 18436
  106.0 80.7 %reduce-scatter.18.cloned.1.call-start = ((), (), s32[]{:S(2)}) async-start(), calls=%async_computation.18 | async-start | bytes 2359296 | tf_op jit(solution)/shard_map/reduce_scatter | solution.py:134
  160.5 61.1 %all-gather.23.cloned.1.call-start = ((), (), s32[]{:S(2)}) async-start(), calls=%async_computation.19 | async-start | bytes 2359296 | tf_op jit(solution)/shard_map/all_gather | solution.py:79
  188.6 3.6 collective-permute-start
  194.2 84.6 %reduce-scatter.20.cloned.1.call-start = ((), (), s32[]{:S(2)}) async-start(), calls=%async_computation.20 | async-start | bytes 2359296 | tf_op jit(solution)/shard_map/reduce_scatter | solution.py:116
  195.3 34.1 %copy-start.51 = (pred[512,512]{0,1:T(8,128)(4,1)}, pred[512,512]{0,1:T(8,128)(4,1)S(1)}, u32[]{:S(2)}) copy-start(pred[512,512]{0,1:T(8,128)(4,1)S(1)} %fusion.394) | copy-start | bytes 786436
  252.5 29.4 %copy-start.122 = (f32[2,768]{1,0:T(2,128)S(1)}, f32[2,768]{1,0:T(2,128)}, u32[]{:S(2)}) copy-start(f32[2,768]{1,0:T(2,128)} %get-tuple-element.191) | copy-start | bytes 18436
  252.5 58.2 %copy-start.111 = (f32[2,1536]{1,0:T(2,128)S(1)}, f32[2,1536]{1,0:T(2,128)}, u32[]{:S(2)}) copy-start(f32[2,1536]{1,0:T(2,128)} %bitcast_convert_fusion) | copy-start | bytes 36868
  252.6 58.1 %all-gather.25.cloned.1.call-start = ((), (), s32[]{:S(2)}) async-start(), calls=%async_computation.21 | async-start | bytes 2359296 | tf_op jit(solution)/shard_map/all_gather | solution.py:125
  283.3 80.3 %reduce-scatter.22.cloned.1.call-start = ((), (), s32[]{:S(2)}) async-start(), calls=%async_computation.22 | async-start | bytes 2359296 | tf_op jit(solution)/shard_map/reduce_scatter | solution.py:134
  337.4 67.4 %all-gather.27.cloned.1.call-start = ((), (), s32[]{:S(2)}) async-start(), calls=%async_computation.23 | async-start | bytes 2359296 | tf_op jit(solution)/shard_map/all_gather | solution.py:79
  367.1 4.0 collective-permute-start.1
  373.1 567.5 %copy-start.12 = (bf16[2,256,768]{2,1,0:T(8,128)(2,1)}, bf16[2,256,768]{2,1,0:T(8,128)(2,1)S(1)}, u32[]{:S(2)}) copy-start(bf16[2,256,768]{2,1,0:T(8,128)(2,1)S(1)} %get-tuple-element.122) | copy-start | bytes 2359300
  373.3 820.0 %copy-start.1 = (bf16[2,2,256,768]{3,2,0,1:T(8,128)(2,1)}, bf16[2,2,256,768]{3,2,0,1:T(8,128)(2,1)S(1)}, u32[]{:S(2)}) copy-start(bf16[2,2,256,768]{3,2,0,1:T(8,128)(2,1)S(1)} %fusion.420) | copy-start | bytes 4718596
  377.2 86.4 %reduce-scatter.24.cloned.1.call-start = ((), (), s32[]{:S(2)}) async-start(), calls=%async_computation.24 | async-start | bytes 2359296 | tf_op jit(solution)/shard_map/reduce_scatter | solution.py:116
  437.4 61.5 %all-gather.29.cloned.1.call-start = ((), (), s32[]{:S(2)}) async-start(), calls=%async_computation.25 | async-start | bytes 2359296 | tf_op jit(solution)/shard_map/all_gather | solution.py:125
  471.5 56.1 %all-gather.31.cloned.1.call-start = ((), (), s32[]{:S(2)}) async-start(), calls=%async_computation.26 | async-start | bytes 2359296 | tf_op jit(solution)/shard_map/all_gather | solution.py:187
  472.1 84.4 %all-gather.51.cloned.1.call-start = ((), (), s32[]{:S(2)}) async-start(), calls=%async_computation.44 | async-start | bytes 2359296 | tf_op jit(solution)/shard_map/all_gather | solution.py:79
  472.8 114.2 %all-gather.35.cloned.1.call-start = ((), (), s32[]{:S(2)}) async-start(), calls=%async_computation.30 | async-start | bytes 2359296 | tf_op jit(solution)/shard_map/all_gather | solution.py:79
  473.4 144.6 %all-gather.43.cloned.1.call-start = ((), (), s32[]{:S(2)}) async-start(), calls=%async_computation.37 | async-start | bytes 2359296 | tf_op jit(solution)/shard_map/all_gather | solution.py:79
  474.0 174.9 %reduce-scatter.26.cloned.1.call-start = ((), (), s32[]{:S(2)}) async-start(), calls=%async_computation.27 | async-start | bytes 2359296 | tf_op jit(solution)/shard_map/reduce_scatter | solution.py:201
  546.8 124.7 %reduce-scatter.42.cloned.1.call-start = ((), (), s32[]{:S(2)}) async-start(), calls=%async_computation.45 | async-start | bytes 2359296 | tf_op jit(solution)/shard_map/reduce_scatter | solution.py:116
  586.5 113.9 %reduce-scatter.30.cloned.1.call-start = ((), (), s32[]{:S(2)}) async-start(), calls=%async_computation.31 | async-start | bytes 2359296 | tf_op jit(solution)/shard_map/reduce_scatter | solution.py:116
  617.7 111.6 %reduce-scatter.36.cloned.1.call-start = ((), (), s32[]{:S(2)}) async-start(), calls=%async_computation.38 | async-start | bytes 2359296 | tf_op jit(solution)/shard_map/reduce_scatter | solution.py:116
  648.8 115.1 %all-gather.33.cloned.1.call-start = ((), (), s32[]{:S(2)}) async-start(), calls=%async_computation.28 | async-start | bytes 2359296 | tf_op jit(solution)/shard_map/all_gather | solution.py:213
  736.6 89.3 %reduce-scatter.28.cloned.1.call-start = ((), (), s32[]{:S(2)}) async-start(), calls=%async_computation.29 | async-start | bytes 2359296 | tf_op jit(solution)/shard_map/reduce_scatter | solution.py:261
  766.3 17.1 slice-start.6
  766.3 17.1 slice-start.7
  783.3 12.8 copy-start.106
  799.7 62.5 %all-gather.37.cloned.1.call-start = ((), (), s32[]{:S(2)}) async-start(), calls=%async_computation.32 | async-start | bytes 2359296 | tf_op jit(solution)/shard_map/all_gather | solution.py:125
  834.8 56.2 %all-gather.39.cloned.1.call-start = ((), (), s32[]{:S(2)}) async-start(), calls=%async_computation.33 | async-start | bytes 2359296 | tf_op jit(solution)/shard_map/all_gather | solution.py:187
  839.3 4.2 collective-permute-start.2
  845.2 91.3 %reduce-scatter.32.cloned.1.call-start = ((), (), s32[]{:S(2)}) async-start(), calls=%async_computation.34 | async-start | bytes 2359296 | tf_op jit(solution)/shard_map/reduce_scatter | solution.py:201
  910.3 64.9 %all-gather.41.cloned.1.call-start = ((), (), s32[]{:S(2)}) async-start(), calls=%async_computation.35 | async-start | bytes 2359296 | tf_op jit(solution)/shard_map/all_gather | solution.py:213
  947.8 29.7 %copy-start.131 = (f32[2,6,512]{2,1,0:T(8,128)S(1)}, f32[2,6,512]{2,1,0:T(8,128)}, u32[]{:S(2)}) copy-start(f32[2,6,512]{2,1,0:T(8,128)} %get-tuple-element.168) | copy-start | bytes 73732
  947.8 89.3 %reduce-scatter.34.cloned.1.call-start = ((), (), s32[]{:S(2)}) async-start(), calls=%async_computation.36 | async-start | bytes 2359296 | tf_op jit(solution)/shard_map/reduce_scatter | solution.py:261
  977.5 17.1 slice-start.3
  977.5 17.1 slice-start.4
  994.5 12.8 copy-start.108
  1010.9 32.1 %copy-start.16 = (bf16[2,256,768]{2,1,0:T(8,128)(2,1)S(1)}, bf16[2,256,768]{2,1,0:T(8,128)(2,1)}, u32[]{:S(2)}) copy-start(bf16[2,256,768]{2,1,0:T(8,128)(2,1)} %reduce-scatter.30.cloned.1.call-done) | copy-start | bytes 2359300
  1010.9 54.9 %all-gather.45.cloned.1.call-start = ((), (), s32[]{:S(2)}) async-start(), calls=%async_computation.39 | async-start | bytes 2359296 | tf_op jit(solution)/shard_map/all_gather | solution.py:125
  1011.5 83.1 %all-gather.53.cloned.1.call-start = ((), (), s32[]{:S(2)}) async-start(), calls=%async_computation.46 | async-start | bytes 2359296 | tf_op jit(solution)/shard_map/all_gather | solution.py:125
  1012.2 111.1 %all-gather.47.cloned.1.call-start = ((), (), s32[]{:S(2)}) async-start(), calls=%async_computation.40 | async-start | bytes 2359296 | tf_op jit(solution)/shard_map/all_gather | solution.py:187
  1047.2 12.6 collective-permute-start.3
  1061.6 33.0 %copy-start.115 = (f32[2,1536]{1,0:T(2,128)S(1)}, f32[2,1536]{1,0:T(2,128)}, u32[]{:S(2)}) copy-start(f32[2,1536]{1,0:T(2,128)} %bitcast_convert_fusion) | copy-start | bytes 36868
  1061.6 125.8 %reduce-scatter.38.cloned.1.call-start = ((), (), s32[]{:S(2)}) async-start(), calls=%async_computation.41 | async-start | bytes 2359296 | tf_op jit(solution)/shard_map/reduce_scatter | solution.py:201
  1152.4 96.9 %all-gather.49.cloned.1.call-start = ((), (), s32[]{:S(2)}) async-start(), calls=%async_computation.42 | async-start | bytes 2359296 | tf_op jit(solution)/shard_map/all_gather | solution.py:213
  1195.8 132.6 %reduce-scatter.44.cloned.1.call-start = ((), (), s32[]{:S(2)}) async-start(), calls=%async_computation.47 | async-start | bytes 2359296 | tf_op jit(solution)/shard_map/reduce_scatter | solution.py:134
  1195.8 21.0 %copy-start.59 = (bf16[2,512,768]{2,1,0:T(8,128)(2,1)S(1)}, bf16[2,512,768]{2,1,0:T(8,128)(2,1)}, u32[]{:S(2)}) copy-start(bf16[2,512,768]{2,1,0:T(8,128)(2,1)} %all-gather.35.cloned.1.call-done) | copy-start | bytes 4718596
  1216.5 120.3 %reduce-scatter.40.cloned.1.call-start = ((), (), s32[]{:S(2)}) async-start(), calls=%async_computation.43 | async-start | bytes 2359296 | tf_op jit(solution)/shard_map/reduce_scatter | solution.py:261
  1251.6 12.9 slice-start.2
  1286.3 14.4 copy-start.55
  1286.3 472.9 %all-reduce.8.cloned.1.call-start = ((), (), s32[]{:S(2)}) async-start(), calls=%async_computation.48 | async-start | bytes 28311552 | tf_op jit(solution)/shard_map/psum | solution.py:379
  1313.4 15.0 copy-start.13
  1313.4 15.0 copy-start.53
  1313.4 23.4 %copy-start.2 = (bf16[2,2,256,768]{3,2,0,1:T(8,128)(2,1)S(1)}, bf16[2,2,256,768]{3,2,0,1:T(8,128)(2,1)}, u32[]{:S(2)}) copy-start(bf16[2,2,256,768]{3,2,0,1:T(8,128)(2,1)} %copy-done.1) | copy-start | bytes 4718596
  1328.4 13.0 copy-start.87
  (192 other events, 786.8 us)
Sparse Core Ops, SparseCore 0:
  14.8 29.9 all-gather.18
  74.8 26.0 reduce-scatter.15
  106.2 27.2 all-gather.20
  160.6 26.0 reduce-scatter.17
  194.3 27.2 all-gather.22
  252.7 26.0 reduce-scatter.19
  283.4 27.2 all-gather.24
  337.5 26.0 reduce-scatter.21
  377.4 27.4 all-gather.26
  437.5 26.0 reduce-scatter.23
  471.6 27.2 all-gather.28
  500.3 27.1 all-gather.30
  529.2 27.1 all-gather.50
  557.9 27.2 all-gather.34
  586.6 27.2 all-gather.42
  616.6 26.0 reduce-scatter.25
  645.4 26.0 reduce-scatter.41
  674.3 26.0 reduce-scatter.29
  703.2 26.0 reduce-scatter.35
  736.7 27.2 all-gather.32
  799.8 26.0 reduce-scatter.27
  834.9 27.2 all-gather.36
  863.7 27.1 all-gather.38
  910.4 26.0 reduce-scatter.31
  947.9 27.2 all-gather.40
  1011.0 26.0 reduce-scatter.33
  1038.5 27.1 all-gather.44
  1067.3 27.2 all-gather.52
  1096.1 27.1 all-gather.46
  1152.5 26.0 reduce-scatter.37
  1195.9 27.2 all-gather.48
  1225.5 26.0 reduce-scatter.43
  1286.4 26.0 reduce-scatter.39
  1318.5 440.6 all-reduce.7
where the time goes:
time: 1790 us; the launch traced here: 1780 us
  waiting for transfers between devices  913 us (51%)
  matrix products  527 us (29%)
  other arithmetic  194 us (11%)
  local copies, waits for them, and re-layouts  71.9 us (4%)
  blocking collectives  46.8 us (3%)
    psum x1, waiting for transfers between devices, local(): lax.psum(totals[0].astype(jnp.bfloat16), 'dp').astype(jnp.float32)  364 us
    reduce_scatter x6, waiting for transfers between devices, layer_forward(): lax.psum_scatter(attn_terms.astype(jnp.bfloat16), 'tensor', scatter_dimen...  149 us
    all_gather x6, waiting for transfers between devices, layer_forward(): mixed_all = lax.all_gather(mixed_low, 'tensor', axis=1, tiled=True)  119 us
    sub x6, matrix products, layer_forward(): shifted = scores - jnp.max(scores, axis=-1, keepdims=True)  78.6 us
    all_gather x6, waiting for transfers between devices, layer_forward(): normed_all = lax.all_gather(normed, 'tensor', axis=1, tiled=True)  73.7 us
    dot_general x3, matrix products, layer_forward(): jnp.einsum('bnf,bfd->bnd', active, drop_weight, preferred_element_type=jn...  59.7 us
    all_gather x3, waiting for transfers between devices, layer_backward(): grad_attn_all = lax.all_gather(grad_attn_low, 'tensor', axis=1, tiled=True)  53.8 us
    dot_general x6, matrix products, layer_forward(): jnp.einsum('bnd,bdf->bnf', mixed_all, lift_weight, preferred_element_type...  52.2 us
  transfers between devices with their start and end apart: 38, of which 30 were waited for; matrix products, arithmetic and copies ran while one was open for 23% of the time, Pallas kernels for 0%

commit v1 on v0

v1 whole, which is shorter than its diff:
```python
from functools import partial

import jax
import jax.numpy as jnp
from jax import lax
from jax.experimental import pallas as pl
from jax.experimental.pallas import tpu as pltpu
from jax.sharding import PartitionSpec as P

HEADS = 12
HEAD_DIM = 64
EPSILON = 1e-06
SCALE = HEAD_DIM ** (-0.5)
FAR = 1e30
CHUNK = 32
AHEAD = 3
HOP = 2
VMEM_LIMIT = 44 * 1024 * 1024
MESH = pl.DeviceIdType.MESH


def swap(value, axis):
    return lax.ppermute(value, axis, [(0, 1), (1, 0)])


def pick(stacked, index, axis=0):
    return lax.dynamic_index_in_dim(stacked, index, axis, keepdims=False)


def masked_distance(lengths, keep_row):
    rows_all = keep_row.shape[0]
    slots = lengths.shape[0]
    positions = jnp.arange(rows_all, dtype=jnp.int32)
    ends = jnp.cumsum(lengths)
    segment = jnp.sum((positions[:, None] >= ends[None, :]).astype(jnp.int32), axis=1)
    following = jnp.arange(1, slots + 1, dtype=jnp.int32)
    item_ids = jnp.arange(slots, dtype=jnp.int32)
    begin = jnp.sum(jnp.where(segment[:, None] == following[None, :], ends[None, :], 0), axis=1)
    length = jnp.sum(jnp.where(segment[:, None] == item_ids[None, :], lengths[None, :], 0), axis=1)
    side = jnp.where(length == 144, 12, jnp.where(length == 225, 15, 20)).astype(jnp.int32)
    offset = positions - begin
    grid_row = (offset // side).astype(jnp.float32)
    column = (offset % side).astype(jnp.float32)
    row_gap = grid_row[:, None] - grid_row[None, :]
    col_gap = column[:, None] - column[None, :]
    distance = jnp.sqrt(row_gap * row_gap + col_gap * col_gap)
    allowed = (segment[:, None] == segment[None, :]) & (
        (keep_row[None, :] == 1) | (positions[:, None] == positions[None, :])
    )
    return jnp.where(allowed, distance, FAR)


def dot(a, b, dims=((1,), (0,))):
    return lax.dot_general(a, b, (dims, ((), ())), preferred_element_type=jnp.float32)


def low(value):
    return value.astype(jnp.bfloat16)


def wide(value):
    return value.astype(jnp.float32)


def shape(dims, dtype=jnp.bfloat16):
    return jax.ShapeDtypeStruct(tuple(dims), dtype)


def row_blocks(count, size=64):
    return [pl.ds(r, size) for r in range(0, count, size)]


def norm_rows(values, gain, shift):
    mean = jnp.mean(values, axis=-1, keepdims=True)
    centred = values - mean
    variance = jnp.mean(centred * centred, axis=-1, keepdims=True)
    return centred * lax.rsqrt(variance + EPSILON) * gain + shift


def norm_rows_back(values, grad, gain):
    mean = jnp.mean(values, axis=-1, keepdims=True)
    centred = values - mean
    variance = jnp.mean(centred * centred, axis=-1, keepdims=True)
    spread = lax.rsqrt(variance + EPSILON)
    unit = centred * spread
    scaled = grad * gain
    along = jnp.mean(scaled * unit, axis=-1, keepdims=True)
    level = jnp.mean(scaled, axis=-1, keepdims=True)
    return spread * (scaled - level - unit * along), grad * unit


def column_sum(value):
    return jnp.sum(value, axis=0, keepdims=True)


def widen_kernel(g_ref, drop, lift, joint, out):
    number = pl.program_id(1)
    part = joint.shape[-1]
    count = pl.num_programs(1)

    @pl.when(number < (count - 2) // 2)
    def _():
        drop[...] = wide(g_ref[...])

    @pl.when((number >= (count - 2) // 2) & (number < count - 2))
    def _():
        lift[...] = wide(g_ref[...])

    @pl.when(number == count - 2)
    def _():
        for i in range(2):
            joint[0, i] = wide(g_ref[0, :, pl.ds(i * part, part)])

    @pl.when(number == count - 1)
    def _():
        for i in range(2):
            joint[0, 2, pl.ds(i * part, part)] = wide(g_ref[0, pl.ds(0, part), pl.ds(i * part, part)])
        out[0] = wide(g_ref[0, pl.ds(part, part)])


def widened(grads, inner, part):
    streams, _, width = grads.shape
    each = inner // width
    block = (1, width, width)
    return pl.pallas_call(
        widen_kernel,
        grid=(streams, 2 * each + 2),
        in_specs=[pl.BlockSpec(block, lambda b, i: (b, i, 0))],
        out_specs=[
            pl.BlockSpec(block, lambda b, i: (b, jnp.minimum(i, each - 1), 0)),
            pl.BlockSpec(block, lambda b, i: (b, 0, jnp.clip(i - each, 0, each - 1))),
            pl.BlockSpec((1, 3, width, part), lambda b, i: (b, 0, 0, 0)),
            pl.BlockSpec((1, part, width), lambda b, i: (b, 0, 0)),
        ],
        out_shape=[
            shape((streams, inner, width), jnp.float32),
            shape((streams, width, inner), jnp.float32),
            shape((streams, 3, width, part), jnp.float32),
            shape((streams, part, width), jnp.float32),
        ],
        compiler_params=pltpu.CompilerParams(vmem_limit_bytes=VMEM_LIMIT),
    )(grads)


class Names:
    def __init__(self, pairs):
        for name, ref in pairs:
            setattr(self, name, ref)


KEPT = ("qkvc", "e", "inv", "normed", "source", "middle", "mixed", "act", "steep", "base")
WEIGHTS = ("drop", "lift", "joint", "out")
GIVEN = ("joint", "out", "small", "lift", "drop")
VECTORS = 6
LOADS = 64


def kept_shapes(s, packs, every, width, part, inner):
    heads = part // HEAD_DIM
    f32 = jnp.float32
    dims = {
        "qkvc": shape((packs, every, 4 * part)),
        "e": shape((packs, heads, every, every)),
        "inv": shape((packs, every, part), f32),
        "normed": shape((packs, every, width)),
        "source": shape((packs, every, width)),
        "middle": shape((packs, every, width), f32),
        "mixed": shape((packs, every, width)),
        "act": shape((packs, every, inner)),
        "steep": shape((packs, every, inner)),
        "base": shape((packs, every, width)),
    }
    if s == 0:
        dims.pop("source")
    return dims


def forward_plan(packs, every, width, part, inner):
    full, f32, bf16 = (packs, every, width), jnp.float32, jnp.bfloat16
    rooms = {
        "joint": ((2, 3, width, part), bf16),
        "out": ((2, part, width), bf16),
        "small_in": ((2, 16, width), bf16),
        "lift": ((2, width, inner), bf16),
        "drop": ((2, inner, width), bf16),
        "dist": ((packs, every, every), f32),
        "rows_in": (full, bf16),
        "base": (full, bf16),
        "dy": (full, bf16),
        "normed": (full, bf16),
        "crossed": (full, bf16),
        "source": (full, bf16),
        "qkvc": ((packs, every, 4 * part), bf16),
        "e": ((part // HEAD_DIM, every, every), bf16),
        "inv": ((packs, every, part), f32),
        "a_mine": (full, bf16),
        "a_peer": (full, bf16),
        "y_mine": (full, bf16),
        "y_peer": (full, bf16),
        "middle": (full, f32),
        "mixed": (full, bf16),
        "act": ((packs, every, inner), bf16),
        "steep": ((packs, every, inner), bf16),
        "scores": ((2, every, every), f32),
        "hidden": ((2, every, 256), f32),
    }
    sem = pltpu.SemaphoreType.DMA
    flags = {
        "w_load": sem((5,)),
        "w_send": sem((5,)),
        "w_recv": sem((5,)),
        "d_load": sem((packs,)),
        "r_load": sem((2, packs)),
        "r_send": sem((2, 2, 2, packs)),
        "r_recv": sem((2, 2, packs)),
        "x_send": sem((2, 2, packs)),
        "x_recv": sem((2, 2, packs)),
        "c_send": sem((packs,)),
        "c_recv": sem((packs,)),
        "store": sem((LOADS,)),
    }
    scratch = [pltpu.VMEM(*spec) for spec in rooms.values()] + list(flags.values())
    return list(rooms) + list(flags), scratch


def forward_kernel(packs, names, *refs):
    refs = list(refs)

    def take(n):
        taken = refs[:n]
        del refs[:n]
        return taken

    slopes, rows_ref, dist_ref = take(3)
    given = dict(zip(GIVEN, take(5)))
    kept = [
        Names(zip([k for k in KEPT if s or k != "source"], take(len(KEPT) - (s == 0)))) for s in range(2)
    ]
    placed = [Names(zip(WEIGHTS, take(4))) for _ in range(2)]
    small_ref, dy_ref, y_ref = take(3)
    w = Names(zip(names, refs))
    core, half = lax.axis_index("section"), lax.axis_index("tensor")
    away = 1 - half
    every, width = w.base.shape[1:]
    rows = every // 2
    part, inner = w.out.shape[1], w.drop.shape[1]
    own = pl.ds(pl.multiple_of(half * rows, rows), rows)
    x_peer = {"tensor": away}
    sibling = {"section": 1 - core}
    early = lax.broadcasted_iota(jnp.int32, (1, 2 * HEAD_DIM), 1) < HEAD_DIM
    across = ((1,), (1,))

    def remote(src, dst, sent, got, target):
        return pltpu.make_async_remote_copy(
            src_ref=src, dst_ref=dst, send_sem=sent, recv_sem=got,
            device_id=target, device_id_type=MESH,
        )

    def weight_load(i):
        return pltpu.make_async_copy(
            given[GIVEN[i]].at[core], getattr(w, room[i]).at[core], w.w_load.at[i]
        )

    def weight_out(i):
        return remote(
            given[GIVEN[i]].at[1 - core], getattr(w, room[i]).at[core], w.w_send.at[i], w.w_recv.at[i], sibling
        )

    def dist_load(m):
        return pltpu.make_async_copy(dist_ref.at[m], w.dist.at[m], w.d_load.at[m])

    room = ("joint", "out", "small_in", "lift", "drop")
    lands = (w.rows_in, w.dy)

    def rows_load(kind, m):
        return pltpu.make_async_copy(rows_ref.at[kind, m], lands[kind].at[m, own], w.r_load.at[kind, m])

    def rows_out(kind, b, t, m):
        side = jnp.where(t == half, 0, 1)
        return remote(
            rows_ref.at[b, m], lands[kind].at[m, own], w.r_send.at[kind, b, side, m], w.r_recv.at[kind, side, m],
            {"section": b, "tensor": t},
        )

    def rows_start(kind, m):
        @pl.when(core == kind)
        def _():
            rows_out(kind, 1 - kind, away, m).start()
            rows_out(kind, kind, away, m).start()
            rows_out(kind, 1 - kind, half, m).start()

    def rows_got(kind, m):
        rows_out(kind, 0, away, m).wait_recv()

        @pl.when(core == kind)
        def _():
            rows_load(kind, m).wait()

        @pl.when(core != kind)
        def _():
            rows_out(kind, 0, half, m).wait_recv()

    def rows_sent(kind, m):
        @pl.when(core == kind)
        def _():
            rows_out(kind, 1 - kind, away, m).wait_send()
            rows_out(kind, kind, away, m).wait_send()
            rows_out(kind, 1 - kind, half, m).wait_send()

    for i in range(len(room)):
        weight_load(i).start()
    for m in range(packs):
        dist_load(m).start()
        for kind in range(2):
            pl.when(core == kind)(lambda: rows_load(kind, m).start())
    barrier = pltpu.get_barrier_semaphore()
    for c, t in [(1 - core, half), (core, away), (1 - core, away)]:
        pl.semaphore_signal(
            barrier, inc=1, device_id={"section": c, "tensor": t}, device_id_type=MESH
        )
    pl.semaphore_wait(barrier, 3)
    rows_start(0, 0)
    for i in range(3):
        weight_out(i).start()
    for m in range(1, packs):
        rows_start(0, m)
    for i in range(3, len(room)):
        weight_out(i).start()

    numbers = iter(range(LOADS))
    pending = {}

    def store(key, src, dst):
        copy = pltpu.make_async_copy(src, dst, w.store.at[next(numbers)])
        copy.start()
        pending[key] = copy

    def free(*key):
        if key in pending:
            pending.pop(key).wait()

    def keep(name, s, m):
        store((name, m), getattr(w, name).at[m], getattr(kept[s], name).at[m])

    def weight_got(name, s):
        i = room.index(name)
        pl.when(core == s)(lambda: weight_load(i).wait())
        pl.when(core != s)(lambda: weight_out(i).wait_recv())
        if name in WEIGHTS:
            store((name, "placed", s), getattr(w, name).at[s], getattr(placed[s], name))

    vectors = [None, None]

    def small_got(s):
        weight_got("small_in", s)
        vectors[s] = wide(w.small_in[s])
        small_ref[s] = vectors[s]

    def row(s, i):
        return vectors[s][i : i + 1]

    def over_x(src, dst, kind, s, m):
        return remote(src, dst, w.x_send.at[kind, s, m], w.x_recv.at[kind, s, m], x_peer)

    def a_copy(s, m):
        return over_x(w.a_mine.at[m], w.a_peer.at[m], 0, s, m)

    def y_copy(m):
        return over_x(w.y_mine.at[m], w.y_peer.at[m], 1, 0, m)

    def crossing(m):
        return remote(w.normed.at[m], w.crossed.at[m], w.c_send.at[m], w.c_recv.at[m], sibling)

    def attention(s, m):
        source = w.source if s else w.normed
        free("qkvc", m)
        w.qkvc[m, :, pl.ds(0, part)] = low(SCALE * dot(w.normed[m], w.joint[s, 0]))
        if s:

            @pl.when(core == 0)
            def _():
                w.source[m] = w.normed[m]

            @pl.when(core == 1)
            def _():
                crossing(m).wait_recv()
                w.source[m] = w.crossed[m]

            keep("source", s, m)
        for i in (1, 2):
            w.qkvc[m, :, pl.ds(i * part, part)] = low(dot(source[m], w.joint[s, i]))
        if s == 0:
            dist_load(m).wait()
        free("inv", m)
        free("e")

        @pl.loop(0, part // (2 * HEAD_DIM))
        def _(pair):
            def lanes(i):
                start = i * part + pair * 2 * HEAD_DIM
                return pl.ds(pl.multiple_of(start, 2 * HEAD_DIM), 2 * HEAD_DIM)

            queries, keys, values = (w.qkvc[m, :, lanes(i)] for i in range(3))
            for side in range(2):
                here = early if side == 0 else jnp.logical_not(early)
                w.scores[side] = dot(jnp.where(here, queries, 0), keys, across)
            for side in range(2):
                head = 2 * pair + side
                here = early if side == 0 else jnp.logical_not(early)
                slope = slopes[head]
                for at in row_blocks(every):
                    value = w.scores[side, at] - slope * w.dist[m, at]
                    expo = jnp.exp(value - jnp.max(value, axis=-1, keepdims=True))
                    w.e[head, at] = low(expo)
                    inverse = 1.0 / jnp.sum(expo, axis=-1, keepdims=True)
                    if side == 0:
                        w.inv[m, at, lanes(0)] = jnp.broadcast_to(inverse, (64, 2 * HEAD_DIM))
                    else:
                        w.inv[m, at, lanes(0)] = jnp.where(here, inverse, w.inv[m, at, lanes(0)])
            sums = [dot(w.e[2 * pair + side], values) for side in range(2)]
            context = jnp.where(early, sums[0], sums[1]) * w.inv[m, :, lanes(0)]
            w.qkvc[m, :, lanes(3)] = low(context)

        if m == 0:
            weight_got("out", s)
        if s:
            a_copy(0, m).wait_send()
        for r in (0, rows):
            at = pl.ds(r, rows)
            w.a_mine[m, at] = low(dot(w.qkvc[m, at, pl.ds(3 * part, part)], w.out[s]))
        a_copy(s, m).start()
        store(("e",), w.e, kept[s].e.at[m])
        keep("qkvc", s, m)
        keep("inv", s, m)

    def feed_forward(s, m):
        base = w.base if s else w.rows_in
        a_copy(s, m).wait_recv()
        for name in ("middle", "mixed", "act", "steep"):
            free(name, m)
        for at in row_blocks(every):
            total = wide(w.a_mine[m, at]) + wide(w.a_peer[m, at])
            value = wide(base[m, at]) + total + row(s, 4)
            w.middle[m, at] = value
            w.mixed[m, at] = low(norm_rows(value, row(s, 1), row(s, 3)))
        if m == 0:
            weight_got("lift", s)
            weight_got("drop", s)
        size = w.hidden.shape[-1]
        for number in range(inner // size):
            lanes = pl.ds(number * size, size)
            at, off = divmod(number * size, width)
            bias = vectors[s][VECTORS + at : VECTORS + at + 1, off : off + size]
            w.hidden[number % 2] = dot(w.mixed[m], w.lift[s, :, lanes])
            for at in row_blocks(every):
                value = w.hidden[number % 2, at] + bias
                below = 0.5 + 0.5 * lax.erf(value * (0.5**0.5))
                density = 0.3989422804014327 * jnp.exp(-0.5 * value * value)
                w.act[m, at, lanes] = low(value * below)
                w.steep[m, at, lanes] = low(below + value * density)
        if s:
            y_copy(m).wait_send()
        for r in (0, rows):
            at = pl.ds(r, rows)
            w.y_mine[m, at] = low(dot(w.act[m, at], w.drop[s]))
        if s == 0:
            y_copy(m).start()
        else:
            store(("y", m), w.y_mine.at[m], y_ref.at[m])
        for name in ("middle", "mixed", "act", "steep"):
            keep(name, s, m)

    def enter(m):
        y_copy(m).wait_recv()
        free("normed", m)
        for at in row_blocks(every):
            total = wide(w.y_mine[m, at]) + wide(w.y_peer[m, at])
            value = low(w.middle[m, at] + total + row(0, 5))
            w.base[m, at] = value
            w.normed[m, at] = low(norm_rows(wide(value), row(1, 0), row(1, 2)))
        pl.when(core == 0)(lambda: crossing(m).start())
        keep("base", 1, m)
        keep("normed", 1, m)

    small_got(0)
    weight_got("joint", 0)
    for m in range(packs):
        rows_got(0, m)
        for at in row_blocks(every):
            w.normed[m, at] = low(norm_rows(wide(w.rows_in[m, at]), row(0, 0), row(0, 2)))
        store(("rows", m), w.rows_in.at[m], kept[0].base.at[m])
        keep("normed", 0, m)
        attention(0, m)
    for m in range(packs):
        feed_forward(0, m)
    small_got(1)
    weight_got("joint", 1)
    for m in range(packs):
        enter(m)
        attention(1, m)
    for m in range(packs):
        rows_start(1, m)
    for m in range(packs):
        feed_forward(1, m)
    for m in range(packs):
        rows_got(1, m)
        store(("dy", m), w.dy.at[m], dy_ref.at[m])
    for i in range(len(room)):
        weight_out(i).wait_send()
    for m in range(packs):
        for kind in range(2):
            rows_sent(kind, m)
        a_copy(1, m).wait_send()
        pl.when(core == 0)(lambda: crossing(m).wait_send())
    for key in list(pending):
        free(*key)


def forward(slopes, held, distances, weights):
    packs, rows, width = held.shape[1:]
    every = 2 * rows
    part, inner = weights[1].shape[1], weights[4].shape[1]
    order = dict(zip(GIVEN, weights))
    kept = [kept_shapes(s, packs, every, width, part, inner) for s in range(2)]
    outs = list(kept[0].values()) + list(kept[1].values())
    outs += [shape(order[name].shape[1:]) for name in WEIGHTS] * 2
    outs += [shape((2, 16, width), jnp.float32), shape((packs, every, width)), shape((packs, every, width))]
    names, scratch = forward_plan(packs, every, width, part, inner)
    anywhere = pl.BlockSpec(memory_space=pl.ANY)
    out_specs = [anywhere] * len(outs)
    out_specs[-3] = pl.BlockSpec(memory_space=pltpu.VMEM)
    found = list(
        pl.pallas_call(
            partial(forward_kernel, packs, names),
            out_shape=outs,
            in_specs=[pl.BlockSpec(memory_space=pltpu.SMEM)] + [anywhere] * 7,
            out_specs=out_specs,
            scratch_shapes=scratch,
            compiler_params=pltpu.CompilerParams(
                collective_id=1, has_side_effects=True, vmem_limit_bytes=60 * 1024 * 1024
            ),
        )(slopes, held, distances, *weights)
    )
    results = []
    for s in range(2):
        layer = {name: found.pop(0) for name in kept[s]}
        layer.setdefault("source", layer["normed"])
        results.append([layer[name] for name in KEPT])
    placed = [[found.pop(0) for _ in WEIGHTS] for _ in range(2)]
    return results, placed, *found


def reducer(line, count, g_refs, o_ref, bufs, sems):
    load_ring, loads_ring, from_y, from_prv, from_nxt, both, mid2, from_y2, res2 = bufs
    load_sem, y_send, y_recv, n_send, n_recv, p_send, p_recv, f_send = sems[:8]
    load2, n2_send, p2_recv, m2_recv, u2_send, u2_recv, a2_send, r2_recv, o2_send = sems[8:17]
    s_send, l_sem, s2_send, l2_sem, f_recv, d_recv, s_recv = sems[17:]
    dp = lax.axis_index("dp")
    core = lax.axis_index("section")
    y, z = dp % 2, dp // 2
    depth = line // 2 - 1
    left = z < line // 2
    step = jnp.where(left, 1, -1)
    edge = jnp.where(left, z, line - 1 - z)
    mine = jnp.where(left, 0, 1)
    total = 2 * count
    slots = from_y.shape[0]
    ring = load_ring.shape[0]
    inner = edge == depth
    outer = jnp.logical_not(inner)

    def device(z_at, y_at, core_at):
        return {"dp": z_at * 2 + y_at, "section": core_at}

    across = device(z, 1 - y, core)
    across_other = device(z, 1 - y, 1 - core)
    sibling = device(z, y, 1 - core)
    nxt = device(z + step, y, core)
    prv = device(z - step, y, core)

    def greet(extra):
        barrier = pltpu.get_barrier_semaphore()
        targets = [across, across_other, sibling, nxt] + extra
        for target in targets:
            pl.semaphore_signal(barrier, inc=1, device_id=target, device_id_type=MESH)

        @pl.when(edge > 0)
        def _():
            pl.semaphore_signal(barrier, inc=1, device_id=prv, device_id_type=MESH)

        pl.semaphore_wait(barrier, len(targets) + jnp.where(edge > 0, 1, 0))

    def send(src, dst, sent, got, target):
        return pltpu.make_async_remote_copy(
            src_ref=src,
            dst_ref=dst,
            send_sem=sent,
            recv_sem=got,
            device_id=target,
            device_id_type=MESH,
        )

    def plus(into, other):
        return (into.astype(jnp.float32) + other.astype(jnp.float32)).astype(into.dtype)

    def guarded(k, body):
        pl.when((k >= 0) & (k < total))(lambda: body(k))

    def by_layer(k, body):
        pl.when(k < count)(lambda: body(g_refs[1], k))
        pl.when(k >= count)(lambda: body(g_refs[0], k - count))

    def stays(k):
        return jnp.where(k < count, 1, 0) == core

    def place(k):
        return jnp.where(k < count, k, k - count)

    def load(k, g_ref=g_refs[0], j=0):
        return pltpu.make_async_copy(g_ref.at[j, y], load_ring.at[k % ring], load_sem.at[k % ring])

    def over_y(k, g_ref=g_refs[0], j=0):
        i = k % slots
        return send(g_ref.at[j, 1 - y], from_y.at[i], y_send.at[i], y_recv.at[i], across)

    def inward(k):
        i = k % slots
        return send(from_y.at[i], from_prv.at[i], n_send.at[i], p_recv.at[i], nxt)

    def middle(k):
        i = k % slots
        return send(from_y.at[i], from_nxt.at[i], n_send.at[i], n_recv.at[i], nxt)

    def outward(k):
        i = k % slots
        return send(from_nxt.at[i], from_nxt.at[i], p_send.at[i], n_recv.at[i], prv)

    def keep(k):
        i = k % slots
        return pltpu.make_async_copy(from_nxt.at[i], o_ref.at[core, place(k), y], l_sem.at[i])

    def hand(k):
        i = k % slots
        return send(from_nxt.at[i], o_ref.at[core, place(k), y], s_send.at[i], s_recv, sibling)

    def back_same(k):
        i = k % slots
        return send(from_nxt.at[i], o_ref.at[core, place(k), y], f_send.at[i], f_recv, across)

    def back_other(k):
        i = k % slots
        return send(from_nxt.at[i], o_ref.at[core, place(k), y], f_send.at[i], d_recv, across_other)

    def begin(k):
        def one(g_ref, j):
            over_y(k, g_ref, j).start()
            load(k, g_ref, j).start()

        by_layer(k, one)

    def pair(k):
        load(k).wait()
        over_y(k).wait()
        i = k % slots
        from_y[i] = plus(from_y[i], load_ring[k % ring])

    def pass_on(k):
        i = k % slots

        @pl.when(edge > 0)
        def _():
            inward(k).wait_recv()
            from_y[i] = plus(from_y[i], from_prv[i])

        pl.when(inner)(lambda: middle(k).start())
        pl.when(outer)(lambda: inward(k).start())

    def finish(k):
        i = k % slots
        middle(k).wait()

        @pl.when(inner)
        def _():
            from_nxt[i] = plus(from_nxt[i], from_y[i])

        pl.when(edge > 0)(lambda: outward(k).start())

        @pl.when(stays(k))
        def _():
            back_same(k).start()
            keep(k).start()

        @pl.when(jnp.logical_not(stays(k)))
        def _():
            back_other(k).start()
            hand(k).start()

    def loads(k, g_ref=g_refs[0], j=0, into=None):
        into = loads_ring.at[k % ring] if into is None else into
        return pltpu.make_async_copy(g_ref.at[j, pl.ds(2, 2)], into, load2.at[k % ring])

    def inwards(k):
        i = k % slots
        return send(both.at[i], both.at[i], n2_send.at[i], p2_recv.at[i], nxt)

    def halve(k):
        i = k % slots
        return send(both.at[i, 1 - mine], mid2.at[i], n2_send.at[i], m2_recv.at[i], nxt)

    def trade(k):
        i = k % slots
        return send(both.at[i, mine], from_y2.at[i], u2_send.at[i], u2_recv.at[i], across)

    def rejoin(k, q):
        i = k % slots
        return send(res2.at[i, q], res2.at[i, q], a2_send.at[i], r2_recv.at[i, q], nxt)

    def outwards(k, q):
        i = k % slots
        return send(res2.at[i, q], res2.at[i, q], o2_send.at[i, q], r2_recv.at[i, q], prv)

    def keep2(k, q):
        i = k % slots
        return pltpu.make_async_copy(
            res2.at[i, q], o_ref.at[core, place(k), 2 + q], l2_sem.at[i, q]
        )

    def hand2(k, q):
        i = k % slots
        return send(res2.at[i, q], o_ref.at[core, place(k), 2 + q], s2_send.at[i, q], s_recv, sibling)

    def spread(k, q):
        pl.when(edge > 0)(lambda: outwards(k, q).start())
        pl.when(stays(k))(lambda: keep2(k, q).start())
        pl.when(jnp.logical_not(stays(k)))(lambda: hand2(k, q).start())

    def begin2(k):
        def one(g_ref, j):
            pl.when(edge == 0)(lambda: loads(k, g_ref, j, both.at[k % slots]).start())
            pl.when(edge > 0)(lambda: loads(k, g_ref, j).start())

        by_layer(k, one)

    def pass_on2(k):
        i = k % slots
        loads(k).wait()

        @pl.when(edge > 0)
        def _():
            inwards(k).wait_recv()
            both[i] = plus(both[i], loads_ring[k % ring])

        pl.when(inner)(lambda: halve(k).start())
        pl.when(outer)(lambda: inwards(k).start())

    def trade2(k):
        i = k % slots
        halve(k).wait()
        both[i, mine] = plus(both[i, mine], mid2[i])
        trade(k).start()

    def settle2(k):
        i = k % slots
        trade(k).wait()
        res2[i, mine] = plus(both[i, mine], from_y2[i])
        rejoin(k, mine).start()
        spread(k, mine)

    def finish2(k):
        @pl.when(inner)
        def _():
            rejoin(k, 1 - mine).wait_recv()
            spread(k, 1 - mine)

        @pl.when(outer)
        def _():
            inwards(k).wait_send()
            for q in range(2):
                rejoin(k, q).wait_recv()
                spread(k, q)

    def retire(k):
        @pl.when(inner)
        def _():
            rejoin(k, mine).wait_send()

        @pl.when(edge > 0)
        def _():
            outward(k).wait_send()
            for q in range(2):
                outwards(k, q).wait_send()

        back_same(k).wait_send()

        @pl.when(stays(k))
        def _():
            keep(k).wait()
            for q in range(2):
                keep2(k, q).wait()

        @pl.when(jnp.logical_not(stays(k)))
        def _():
            hand(k).wait_send()
            for q in range(2):
                hand2(k, q).wait_send()

    span = AHEAD + HOP * (2 * depth + 3) + 1

    def ticks(first, last):
        @pl.loop(first, last)
        def _(tick):
            now = tick - AHEAD
            guarded(tick - span, retire)
            guarded(tick, begin)
            guarded(now, pair)
            guarded(tick - HOP * edge, begin2)
            guarded(now - HOP * edge, pass_on)
            guarded(now - HOP * edge, pass_on2)

            @pl.when(inner)
            def _():
                guarded(now - HOP * (depth + 1), trade2)
                guarded(now - HOP * (depth + 2), settle2)

            guarded(now - HOP * (2 * depth + 1 - edge), finish)
            guarded(now - HOP * (2 * depth + 3 - edge), finish2)

    def drain():
        group = o_ref.at[0, :, 0]
        groups = o_ref.at[0, :, pl.ds(0, 3)]
        pltpu.make_async_copy(group, group, f_recv).wait()
        pltpu.make_async_copy(group, group, d_recv).wait()
        pltpu.make_async_copy(groups, groups, s_recv).wait()

    return greet, ticks, drain, total + span


def reducer_scratch(line, rows, width):
    slots = AHEAD + HOP * (line + 1) + 3
    ring = AHEAD + 1

    def room(*lead):
        return pltpu.VMEM(lead + (rows, width), jnp.bfloat16)

    def sems(*dims):
        return pltpu.SemaphoreType.DMA(dims)

    bufs = [room(ring), room(ring, 2)] + [room(slots)] * 3 + [room(slots, 2)]
    bufs += [room(slots)] * 2 + [room(slots, 2)]
    many, twice = sems(slots), sems(slots, 2)
    flags = [sems(ring)] + [many] * 7 + [sems(ring)] + [many] * 6 + [twice] * 2
    return bufs, flags + [many] * 2 + [twice] * 2 + [pltpu.SemaphoreType.DMA] * 3


BUFS, SEMS = 9, 24


def reduce_kernel(line, count, g_zero, g_one, o_ref, *refs):
    greet, ticks, drain, length = reducer(
        line, count, (g_zero, g_one), o_ref, refs[:BUFS], refs[BUFS:]
    )
    greet([])
    ticks(0, length)
    drain()


def reduce_over_dp(grads, line):
    count, _, rows, width = grads[0].shape
    bufs, sems = reducer_scratch(line, rows, width)
    return pl.pallas_call(
        partial(reduce_kernel, line, count),
        out_shape=shape((2,) + grads[0].shape),
        in_specs=[pl.BlockSpec(memory_space=pl.ANY)] * 2,
        out_specs=pl.BlockSpec(memory_space=pl.ANY),
        scratch_shapes=bufs + sems,
        compiler_params=pltpu.CompilerParams(
            collective_id=0, has_side_effects=True, vmem_limit_bytes=56 * 1024 * 1024
        ),
    )(*grads)


def backward_scratch(packs, rows, width, part, inner, block):
    full, f32 = (packs, 2 * rows, width), jnp.float32
    bf16 = jnp.bfloat16
    plan = {
        "drop": ((inner, width), bf16),
        "lift": ((width, inner), bf16),
        "joint": ((3, width, part), bf16),
        "out": ((part, width), bf16),
        "dy": (full, bf16),
        "wide_a": ((packs, 2 * rows, inner), bf16),
        "wide_b": ((packs, 2 * rows, inner), bf16),
        "narrow": (full, bf16),
        "source": (full, bf16),
        "dm_mine": (full, bf16),
        "dm_peer": (full, bf16),
        "dn_mine": (full, bf16),
        "dn_peer": (full, bf16),
        "crossed": (full, bf16),
        "middle": (full, f32),
        "dmid": (full, f32),
        "da": (full, bf16),
        "inv": ((packs, 2 * rows, part), f32),
        "base": (full, bf16),
        "ends": ((packs, rows, width), f32),
        "ends_mine": ((packs, rows, width), bf16),
        "ends_peer": ((packs, rows, width), bf16),
        "dx": ((packs, rows, width), bf16),
        "e": ((2, 2, 2 * rows, 2 * rows), bf16),
        "dc": ((2 * rows, part), f32),
        "dprob": ((2, 2 * rows, 2 * rows), f32),
        "ds": ((2, 2 * rows, 2 * rows), bf16),
        "staged": ((3, 2, 4, block // 8, width), bf16),
        "sums": ((2, 8, width), f32),
        "sums_peer": ((2, 8, width), f32),
        "tail": ((4, block // 8, width), bf16),
    }
    sem = pltpu.SemaphoreType.DMA
    flags = {
        "load": sem((LOADS,)),
        "e_load": sem((2,)),
        "x_send": sem((2, 2, packs)),
        "x_recv": sem((2, 2, packs)),
        "c_send": sem((packs,)),
        "c_recv": sem((packs,)),
        "g_store": sem((3,)),
        "t_store": sem((2,)),
        "v_send": sem((2,)),
        "v_recv": sem((2,)),
        "y_send": sem((packs,)),
        "y_recv": sem((packs,)),
        "o_keep": sem((1,)),
        "o_send": sem((1,)),
        "o_recv": sem((1,)),
    }
    return list(plan) + list(flags), [pltpu.VMEM(*spec) for spec in plan.values()] + list(flags.values())


def backward_kernel(line, count, packs, inside, names, *refs):
    refs = list(refs)

    def take(n):
        taken = refs[:n]
        del refs[:n]
        return taken

    small, dy_in, y_in = take(3)
    weights = [Names(zip(WEIGHTS, take(4))) for _ in range(2)]
    kept = [Names(zip(KEPT, take(len(KEPT)))) for _ in range(2)]
    edges_ref, *g_refs = take(3)
    o_ref = take(1)[0] if inside else None
    w = Names(zip(names, take(len(names))))
    core, half = lax.axis_index("section"), lax.axis_index("tensor")
    every, width = w.dy.shape[1:]
    rows = every // 2
    part, inner = w.out.shape[0], w.drop.shape[0]
    block = 8 * w.tail.shape[1]
    pairs = part // (2 * HEAD_DIM)
    x_peer = {"tensor": 1 - half}
    sibling = {"section": 1 - core}
    own = pl.multiple_of(half * rows, rows)
    theirs = pl.multiple_of((1 - half) * rows, rows)
    early = lax.broadcasted_iota(jnp.int32, (1, 2 * HEAD_DIM), 1) < HEAD_DIM
    numbers = iter(range(LOADS))
    down, across = ((0,), (0,)), ((1,), (1,))

    def fetch(src, dst):
        copy = pltpu.make_async_copy(src, dst, w.load.at[next(numbers)])
        copy.start()
        return copy

    def remote(src, dst, sent, got, target):
        return pltpu.make_async_remote_copy(
            src_ref=src, dst_ref=dst, send_sem=sent, recv_sem=got,
            device_id=target, device_id_type=MESH,
        )

    def over_x(src, dst, kind, s, m):
        return remote(src, dst, w.x_send.at[kind, s, m], w.x_recv.at[kind, s, m], x_peer)

    pending = {}

    def ask(key, src, dst):
        pending[key] = fetch(src, dst)

    def got(key):
        pending.pop(key).wait()

    def ask_layer(s):
        for name in ("drop", "lift"):
            ask(name, getattr(weights[s], name), getattr(w, name))

    def ask_rows(s):
        for m in range(packs):
            ask(("steep", m), kept[s].steep.at[m], w.wide_a.at[m])
            ask(("mixed", m), kept[s].mixed.at[m], w.narrow.at[m])

    def ask_attention(s):
        for name in ("joint", "out"):
            ask(name, getattr(weights[s], name), getattr(w, name))
        for m in range(packs):
            ask(("middle", m), kept[s].middle.at[m], w.middle.at[m])
            ask(("inv", m), kept[s].inv.at[m], w.inv.at[m])

    for m in range(packs):
        ask(("dy", m), dy_in.at[m], w.dy.at[m])
        ask(("ends", m), y_in.at[m, pl.ds(own, rows)], w.ends_mine.at[m])
    ask_layer(1)
    ask_rows(1)
    ask_attention(1)

    clock, ready = [0], [0]
    if inside:
        greet, run_ticks, drain, length = reducer(
            line, count, g_refs, o_ref, refs[:BUFS], refs[BUFS:]
        )
        greet([x_peer])

        def ticks(n):
            n = min(n, ready[0] - clock[0])
            if n > 0:
                run_ticks(clock[0], clock[0] + n)
                clock[0] += n
    else:
        barrier = pltpu.get_barrier_semaphore()
        for target in (x_peer, sibling):
            pl.semaphore_signal(barrier, inc=1, device_id=target, device_id_type=MESH)
        pl.semaphore_wait(barrier, 2)

        def ticks(n):
            pass

    def add_sums(s, m, row, value):
        at = pl.ds(row, 1)
        w.sums[s, at] = value if m == 0 else w.sums[s, at] + value

    stores = [None, None, None]
    stored = [0]

    def emit(s, number, fill):
        slot = stored[0] % 3
        stored[0] += 1
        if stores[slot] is not None:
            stores[slot].wait()
        fill(slot)
        stores[slot] = pltpu.make_async_copy(
            w.staged.at[slot], g_refs[s].at[pl.ds(2 * number, 2)], w.g_store.at[slot]
        )
        stores[slot].start()

    def settle_stores():
        for slot in range(3):
            if stores[slot] is not None:
                stores[slot].wait()
                stores[slot] = None

    def put(slot, value, first=0, lanes=slice(None)):
        step = block // 8
        per = 4 * step
        for r in range(0, value.shape[0], step):
            at = first + r
            w.staged[slot, at // per, at % per // step, :, lanes] = low(value[r : r + step])

    def product(lefts, rights):
        return sum(dot(a[...], b[...], down) for a, b in zip(lefts, rights))

    dm = [[over_x(w.dm_mine.at[m], w.dm_peer.at[m], 0, s, m) for m in range(packs)] for s in range(2)]
    dn = [
        [
            over_x(
                w.dn_mine.at[m, pl.ds(theirs, rows)],
                w.dn_peer.at[m, pl.ds(0, rows)],
                1, 0, m,
            )
            for m in range(packs)
        ],
        [over_x(w.dn_mine.at[m], w.dn_peer.at[m], 1, 1, m) for m in range(packs)],
    ]

    def far_copy(m):
        return remote(w.dm_mine.at[m], w.crossed.at[m], w.c_send.at[m], w.c_recv.at[m], sibling)

    def feed_forward(s, m):
        got(("steep", m))
        if s == 0:
            pl.when(core == 1)(lambda: far_copy(m).wait_send())
        size = 256
        for number in range(inner // size):
            lanes = pl.ds(number * size, size)
            grad = dot(w.dy[m], w.drop[lanes], across) * wide(w.wide_a[m, :, lanes])
            grad = low(grad)
            w.wide_b[m, :, lanes] = grad
            total = column_sum(wide(grad))
            at = number * size
            spot = (s, pl.ds(VECTORS + at // width, 1), pl.ds(at % width, size))
            w.sums[spot] = total if m == 0 else w.sums[spot] + total
        ask(("act", m), kept[s].act.at[m], w.wide_a.at[m])
        add_sums(s, m, 5, 0.5 * column_sum(wide(w.dy[m])))
        for r in (0, rows):
            at = pl.ds(r, rows)
            w.dm_mine[m, at] = low(dot(w.wide_b[m, at], w.lift[...], across))
        dm[s][m].start()

    def feed_forward_weights(s, spread):
        for m in range(packs):
            got(("act", m))
            got(("mixed", m))
        number = 0
        for first in range(0, inner, block):
            lanes = pl.ds(first, block)
            value = product([w.wide_a.at[m, :, lanes] for m in range(packs)], [w.dy.at[m] for m in range(packs)])
            emit(s, number, lambda slot: put(slot, value))
            number += 1
            if spread and number % 3 == 0:
                ticks(spread)
        for column in range(0, inner, width):
            for first in range(0, width, block):
                value = product(
                    [w.narrow.at[m, :, pl.ds(first, block)] for m in range(packs)],
                    [w.wide_b.at[m, :, pl.ds(column, width)] for m in range(packs)],
                )
                emit(s, number, lambda slot: put(slot, value))
                number += 1
                if spread and number % 3 == 0:
                    ticks(spread)
        settle_stores()
        ready[0] = (0 if s else count) + 2 * number
        for m in range(packs):
            ask(("qkvc", m), kept[s].qkvc.at[m], w.wide_a.at[m])
            ask(("normed", m), kept[s].normed.at[m], w.narrow.at[m])
            if s:
                ask(("source", m), kept[s].source.at[m], w.source.at[m])
        ask_e(s, 0)

    def e_copy(s, number):
        m, pair = divmod(number, pairs)
        return pltpu.make_async_copy(
            kept[s].e.at[m, pl.ds(2 * pair, 2)], w.e.at[number % 2], w.e_load.at[number % 2]
        )

    def ask_e(s, number):
        if number < packs * pairs:
            e_copy(s, number).start()

    def attention(s, m, spread, between=None):
        if m == 0:
            got("out")
        got(("middle", m))
        if s:
            got(("ends", m))
            for r in range(0, rows, 32):
                at = pl.ds(r, 32)
                mine = w.middle[m, pl.ds(pl.multiple_of(own + r, 32), 32)]
                w.ends[m, at] = mine + wide(w.ends_mine[m, at]) + small[1, pl.ds(5, 1)]
        dm[s][m].wait()
        totals = [0.0, 0.0, 0.0]
        for at in row_blocks(every, 32):
            grad = wide(w.dm_mine[m, at]) + wide(w.dm_peer[m, at])
            pulled, along = norm_rows_back(w.middle[m, at], grad, small[s, pl.ds(1, 1)])
            through = wide(w.dy[m, at]) + pulled
            w.dmid[m, at] = through
            da = low(through)
            w.da[m, at] = da
            for i, piece in enumerate((along, grad, wide(da))):
                totals[i] = totals[i] + column_sum(piece)
        for i, row in enumerate((1, 3, 4)):
            add_sums(s, m, row, 0.5 * totals[i])
        ticks(spread)
        got(("inv", m))
        w.dc[...] = dot(w.da[m], w.out[...], across) * w.inv[m]
        got(("qkvc", m))
        for pair in range(pairs):
            number = m * pairs + pair
            e_copy(s, number).wait()
            ask_e(s, number + 1)
            e_ref = w.e.at[number % 2]

            def lanes(i):
                return pl.ds(i * part + pair * 2 * HEAD_DIM, 2 * HEAD_DIM)

            queries, keys, values = (w.wide_a[m, :, lanes(i)] for i in range(3))
            grad = low(w.dc[:, lanes(0)])
            for side in range(2):
                here = early if side == 0 else jnp.logical_not(early)
                w.dprob[side] = dot(jnp.where(here, grad, 0), values, across)
            for side in range(2):
                here = early if side == 0 else jnp.logical_not(early)
                for at in row_blocks(every):
                    level = jnp.where(here, w.dc[at, lanes(0)] * wide(w.wide_a[m, at, lanes(3)]), 0.0)
                    level = jnp.sum(level, axis=-1, keepdims=True)
                    w.ds[side, at] = low(wide(e_ref[side, at]) * (w.dprob[side, at] - level))
            dv = [dot(e_ref[side], grad, down) for side in range(2)]
            w.wide_b[m, :, lanes(2)] = low(jnp.where(early, dv[0], dv[1]))
            dk = [dot(w.ds[side], queries, down) for side in range(2)]
            w.wide_b[m, :, lanes(1)] = low(jnp.where(early, dk[0], dk[1]))
            dq = [dot(w.ds[side], keys) for side in range(2)]
            w.wide_b[m, :, lanes(0)] = low(SCALE * jnp.where(early, dq[0], dq[1]))
            ticks(spread)
            if between is not None and pair == 0:
                between()
        if m == 0:
            got("joint")
        if s == 0:
            dn[1][m].wait_send()
        for r in (0, rows):
            at = pl.ds(r, rows)
            dq, dk, dv = (w.wide_b[m, at, pl.ds(i * part, part)] for i in range(3))
            far = dot(dk, w.joint[1], across) + dot(dv, w.joint[2], across)
            near = dot(dq, w.joint[0], across)
            if s:
                w.dm_mine[m, at] = low(far)
                w.middle[m, at] = near + jnp.where(core == 0, far, 0.0)
            else:
                w.dn_mine[m, at] = low(near + far)
        if s:
            pl.when(core == 1)(lambda: far_copy(m).start())
        else:
            dn[0][m].start()

    def join(m):
        pl.when(core == 0)(lambda: far_copy(m).wait_recv())
        for at in row_blocks(every, 32):
            there = jnp.where(core == 0, wide(w.crossed[m, at]), 0.0)
            w.dn_mine[m, at] = low(w.middle[m, at] + there)
        dn[1][m].start()

    def attention_weights(s, spread):
        for m in range(packs):
            got(("normed", m))
            if s:
                got(("source", m))
        normed = [w.narrow.at[m] for m in range(packs)]
        source = [w.source.at[m] for m in range(packs)] if s else normed
        dq, dk, dv = (
            [w.wide_b.at[m, :, pl.ds(i * part, part)] for m in range(packs)] for i in range(3)
        )
        context = [w.wide_a.at[m, :, pl.ds(3 * part, part)] for m in range(packs)]
        da = [w.da.at[m] for m in range(packs)]
        number = 2 * inner // block
        for first in range(0, width, block):
            at = pl.ds(first, block)
            query = product([n.at[:, at] for n in normed], dq)
            key = product([n.at[:, at] for n in source], dk)

            def both(slot):
                put(slot, query, 0, pl.ds(0, part))
                put(slot, key, 0, pl.ds(part, part))

            emit(s, number, both)
            number += 1
            ticks(spread)
        size = 128
        per = block // size
        strips = [("value", r) for r in range(0, part, size)] + [("out", r) for r in range(0, part, size)]
        for first in range(0, len(strips), per):
            group = strips[first : first + per]

            def fill(slot):
                for i, (kind, r) in enumerate(group):
                    if kind == "value":
                        for side in range(width // part):
                            at = pl.ds(side * part + r, size)
                            value = product([n.at[:, at] for n in source], dv)
                            put(slot, value, i * size, pl.ds(side * part, part))
                    else:
                        value = product([c.at[:, pl.ds(r, size)] for c in context], da)
                        put(slot, value, i * size)

            emit(s, number, fill)
            number += 1
            ticks(spread)
        settle_stores()
        ready[0] = (0 if s else count) + 2 * number

    def leave(s, m):
        dn[s][m].wait_recv()
        got(("base", m))
        totals = [0.0, 0.0]
        for r in range(0, every if s else rows, 32):
            peer, mine = pl.ds(r, 32), pl.ds(r if s else pl.multiple_of(own + r, 32), 32)
            grad = wide(w.dn_mine[m, mine]) + wide(w.dn_peer[m, peer])
            pulled, along = norm_rows_back(wide(w.base[m, peer]), grad, small[s, pl.ds(0, 1)])
            result = low(w.dmid[m, mine] + pulled)
            if s:
                w.dy[m, peer] = result
            else:
                w.dx[m, peer] = result
            for i, piece in enumerate((along, grad)):
                totals[i] = totals[i] + column_sum(piece)
        scale = 0.5 if s else 1.0
        add_sums(s, m, 0, scale * totals[0])
        add_sums(s, m, 2, scale * totals[1])

    def vectors(s):
        return remote(w.sums.at[s], w.sums_peer.at[s], w.v_send.at[s], w.v_recv.at[s], x_peer)

    def tail_store(s):
        return pltpu.make_async_copy(w.tail, g_refs[s].at[count - 1], w.t_store.at[s])

    def finish_vectors(s):
        vectors(s).wait()
        row = lax.broadcasted_iota(jnp.int32, (8, 1), 0)
        total = w.sums[s] + jnp.where(row < VECTORS, w.sums_peer[s], 0.0)
        if s:
            w.tail[...] = jnp.zeros(w.tail.shape, w.tail.dtype)
        pad = jnp.zeros((w.tail.shape[1] - 8, width), jnp.float32)
        w.tail[0] = low(jnp.concatenate([total, pad]))
        tail_store(s).start()
        tail_store(s).wait()
        ready[0] = count if s else 2 * count

    def ends_copy(m):
        return remote(
            y_in.at[m, pl.ds(theirs, rows)], w.ends_peer.at[m], w.y_send.at[m], w.y_recv.at[m], x_peer
        )

    def ends(m):
        ends_copy(m).wait()
        for at in row_blocks(rows, 32):
            w.ends_mine[m, at] = low(w.ends[m, at] + wide(w.ends_peer[m, at]))

    def edges_keep(src, b):
        return pltpu.make_async_copy(src, edges_ref.at[b], w.o_keep.at[0])

    def edges_hand(src, b):
        return remote(src, edges_ref.at[b], w.o_send.at[0], w.o_recv.at[0], sibling)

    def ask_base(s):
        for m in range(packs):
            if s:
                ask(("base", m), kept[s].base.at[m], w.base.at[m])
            else:
                ask(("base", m), kept[s].base.at[m, pl.ds(own, rows)], w.base.at[m, pl.ds(0, rows)])

    for s in (1, 0):
        if s:
            for m in range(packs):
                got(("dy", m))
        got("drop")
        got("lift")
        for m in range(packs):
            feed_forward(s, m)
            if not s:
                ticks(2)
        if not s:
            finish_vectors(1)
            for m in range(packs):
                ends(m)
            pl.when(core == 0)(lambda: edges_hand(w.ends_mine, 0).start())
            pl.when(core == 1)(lambda: edges_keep(w.ends_mine, 1).start())
        ask_base(s)
        if s:
            ask_layer(0)
            for m in range(packs):
                ends_copy(m).start()
        feed_forward_weights(s, 0 if s else 2)
        for m in range(packs):
            attention(s, m, 2, partial(join, m - 1) if s and m else None)
        if s:
            join(packs - 1)
        if s:
            ask_attention(0)
        attention_weights(s, 1)
        if s:
            ask_rows(0)
        for m in range(packs):
            leave(s, m)
            if s:
                ticks(2)
        vectors(s).start()
    finish_vectors(0)
    pl.when(core == 0)(lambda: edges_keep(w.dx, 0).start())
    pl.when(core == 1)(lambda: edges_hand(w.dx, 1).start())
    if inside:
        run_ticks(clock[0], length)
        drain()
    for m in range(packs):
        dn[0][m].wait_send()
    edges_keep(w.dx, 0).wait()
    edges_hand(w.dx, 0).wait()


def backward(line, small, dy, ends, weights, kept, inside):
    packs, every, width = dy.shape
    rows = every // 2
    inner, part = weights[0][0].shape[0], weights[0][3].shape[0]
    block = 8 * CHUNK
    count = (2 * inner + 4 * part) // (4 * CHUNK) + 1
    chunks = shape((count, 4, CHUNK, width))
    args = [small, dy, ends] + [a for s in range(2) for a in weights[s]] + [a for s in range(2) for a in kept[s]]
    anywhere = pl.BlockSpec(memory_space=pl.ANY)
    outs = [shape((2, packs, rows, width)), chunks, chunks]
    if inside:
        outs.append(shape((2,) + chunks.shape))
    names, scratch = backward_scratch(packs, rows, width, part, inner, block)
    if inside:
        bufs, sems = reducer_scratch(line, CHUNK, width)
        scratch = scratch + bufs + sems
    return pl.pallas_call(
        partial(backward_kernel, line, count, packs, inside, names),
        out_shape=outs,
        in_specs=[pl.BlockSpec(memory_space=pltpu.VMEM)] + [anywhere] * (len(args) - 1),
        out_specs=[anywhere] * len(outs),
        scratch_shapes=scratch,
        compiler_params=pltpu.CompilerParams(
            collective_id=2, has_side_effects=True, vmem_limit_bytes=62 * 1024 * 1024
        ),
    )(*args)


def local(
    edges_in,
    joint_weight,
    output_weight,
    lift_weight,
    lift_bias,
    drop_weight,
    norm_gains,
    norm_shifts,
    branch_biases,
    item_lengths,
    key_keep,
):
    half = lax.axis_index("tensor")
    held = edges_in[0]
    packs, _, width = held.shape[1:]
    part = joint_weight.shape[-1]
    inner = lift_weight.shape[-1]
    heads = part // HEAD_DIM
    head_ids = wide(half * heads + jnp.arange(heads, dtype=jnp.int32))
    slopes = jnp.power(2.0, -8.0 * (head_ids + 1.0) / HEADS)

    small = jnp.concatenate(
        [norm_gains[0], norm_shifts[0], branch_biases[0], lift_bias[0].reshape(2, -1, width)], axis=1
    )
    small = jnp.concatenate([small, jnp.zeros((2, 16 - small.shape[1], width), small.dtype)], axis=1)
    distances = jnp.stack(
        [masked_distance(item_lengths[0, m], key_keep[0, m]) for m in range(packs)]
    )
    given = (joint_weight[0], output_weight[0], small, lift_weight[0], drop_weight[0])
    kept, weights, small, dy, ends = forward(slopes, held, distances, given)
    line = lax.axis_size("dp") // 2
    inside = line == 4
    edges_out, *grads = backward(line, small, dy, ends, weights, kept, inside)
    grads = grads[2] if inside else reduce_over_dp(grads, line)
    grads = grads.reshape(2, -1, width)
    weight_rows = 2 * inner + 4 * part
    drop_grad, lift_grad, joint_grad, output_grad = widened(grads, inner, part)
    vectors = wide(grads[:, weight_rows : weight_rows + 6])
    lift_total = wide(grads[:, weight_rows + 6 : weight_rows + 6 + inner // width]).reshape(2, inner)
    return (
        edges_out[None],
        joint_grad[None],
        output_grad[None],
        lift_grad[None],
        lift_total[None],
        drop_grad[None],
        vectors[None, :, 0:2],
        vectors[None, :, 2:4],
        vectors[None, :, 4:6],
    )


def solution(mesh):
    in_specs = (
        P("section", None, None, ("dp", "tensor"), None),
        P("section", None, None, None, "tensor"),
        P("section", None, "tensor", None),
        P("section", None, None, "tensor"),
        P("section", None, "tensor"),
        P("section", None, "tensor", None),
        P("section", None, None, None),
        P("section", None, None, None),
        P("section", None, None, None),
        P("dp", None, None),
        P("dp", None, None),
    )
    out_specs = (
        P("section", None, None, ("dp", "tensor"), None),
        P("section", None, None, None, "tensor"),
        P("section", None, "tensor", None),
        P("section", None, None, "tensor"),
        P("section", None, "tensor"),
        P("section", None, "tensor", None),
        P("section", None, None, None),
        P("section", None, None, None),
        P("section", None, None, None),
    )
    return jax.shard_map(local, mesh=mesh, in_specs=in_specs, out_specs=out_specs, check_vma=False)
```

time: 1790 us -> 470 us (0.26)
  waiting for transfers between devices: 913 us -> 0 us
  matrix products: 527 us -> 0 us
  Pallas kernels: 0 us -> 452 us
  other arithmetic: 194 us -> 6.79 us
  local copies, waits for them, and re-layouts: 71.9 us -> 5.84 us
  blocking collectives: 46.8 us -> 0 us
    pallas_call x0 -> x3, Pallas kernels: none -> 452 us  [the longest x1 294 us: backward(): pl.pallas_call(partial(backward_kernel, line, count, packs, inside, names...]
    dot_general x87 -> x0, matrix products: 448 us -> none  [the longest x3 59.7 us: layer_forward(): jnp.einsum('bnf,bfd->bnd', active, drop_weight, preferred_element_type=jn...]
    psum x1 -> x0, waiting for transfers between devices: 364 us -> none  [local(): lax.psum(totals[0].astype(jnp.bfloat16), 'dp').astype(jnp.float32)]
    reduce_scatter x15 -> x0, waiting for transfers between devices: 271 us -> none  [the longest x6 149 us: layer_forward(): lax.psum_scatter(attn_terms.astype(jnp.bfloat16), 'tensor', scatter_dimen...]
    all_gather x18 -> x0, waiting for transfers between devices: 269 us -> none  [the longest x6 119 us: layer_forward(): mixed_all = lax.all_gather(mixed_low, 'tensor', axis=1, tiled=True)]
    sub x6 -> x0, matrix products: 78.6 us -> none  [layer_forward(): shifted = scores - jnp.max(scores, axis=-1, keepdims=True)]
    reduce_sum x34 -> x3, other arithmetic: 63 us -> 0.28 us  [the longest x2 0.17 us: masked_distance(): jnp.sum((positions[:, None] >= ends[None, :]).astype(jnp.int32), axis=1)]
    psum x2 -> x0, blocking collectives: 46.8 us -> none  [the longest x1 39.4 us: local(): lax.psum(totals[3].astype(jnp.bfloat16), 'dp').astype(jnp.float32)]
  transfers between devices with their start and end apart: 38 -> 0, of which waited for: 30 -> 0; matrix products, arithmetic and copies ran while one was open for 23% -> 0% of each run, Pallas kernels for 0% -> 0%
where the time goes in v1:
time: 470 us; the launch traced here: 466 us
  Pallas kernels  452 us (96%)
  other arithmetic  6.79 us (1%)
  local copies, waits for them, and re-layouts  5.84 us (1%)
    pallas_call x1, Pallas kernels, backward(): pl.pallas_call(partial(backward_kernel, line, count, packs, inside, names...  294 us
    pallas_call x1, Pallas kernels, forward(): pl.pallas_call(partial(forward_kernel, packs, names), out_shape=outs, in_...  139 us
    pallas_call x1, Pallas kernels, widened(): pl.pallas_call(widen_kernel, grid=(streams, 2 * each + 2), in_specs=[pl.B...  19.1 us

profile of v1, /device:TPU:0, one launch (start us, length us, event | category | flops | bytes accessed | tf_op | source)
XLA Modules:
  0.0 465.6 jit_solution(6584930749469009679)
XLA Ops:
  0.6 0.5 multiply_power_fusion.refs_0_
  1.2 0.8 compare_reduce_fusion.1
  2.0 0.8 slice_bitcast_fusion.4
  2.7 0.2 reduce-window.17
  2.9 0.2 reduce-window.16
  3.1 0.1 convert_reduce_fusion.1
  3.2 0.1 convert_reduce_fusion
  3.2 0.1 select_reduce_fusion.3
  3.4 0.1 fusion.4
  3.5 0.1 fusion.7
  3.6 0.1 fusion.5
  3.7 0.7 reshape_squeeze.3
  4.5 2.0 concatenate.3.refs_5_
  6.4 0.7 sqrt_select_fusion.1
  7.2 0.7 sqrt_select_fusion
  7.9 1.5 pad_maximum_fusion.refs_2_
  9.4 138.7 %shard_map.178 = (bf16[2,512,1536]{2,1,0:T(8,128)(2,1)}, bf16[2,6,512,512]{3,2,1,0:T(8,128)(2,1)}, f32[2,512,384]{2,1,0:T(8,128)}, bf16[2,512,768]{2,1,0:T(8,128...) custom-call(f32[6]{0:T(128)} %multiply_power_fusion.refs_0_, ...), custom_call_target="tpu_custom_call" | custom-call | tf_op jit(solution)/shard_map/pallas_call | solution.py:533
  148.1 294.3 %shard_map.179 = (bf16[2,2,256,768]{3,2,1,0:T(8,128)(2,1)}, bf16[37,4,32,768]{3,2,1,0:T(8,128)(2,1)}, bf16[37,4,32,768]{3,2,1,0:T(8,128)(2,1)}, bf16[2,37,4,32,768]{4,3,2,1,0:T(8,128)(2,1)}) custom-call(f32[2,16,768]{2,1,0:T(8,128)} %get-tuple-element.45.refs_0_, bf16[2,512,768]{2,1,0:T(8,128)(2,1)} %get-tuple-element.46.refs_1_, ...), custom_call_target="tpu_custom_call" | custom-call | tf_op jit(solution)/shard_map/pallas_call | solution.py:1399
  442.4 0.7 slice_convert_fusion.1
  443.2 0.6 reshape.613
  443.8 0.7 slice_convert_fusion
  444.5 0.6 slice_bitcast_fusion
  445.2 0.0 copy-start
  445.2 19.1 %shard_map.180 = (f32[2,1536,768]{2,1,0:T(8,128)}, f32[2,768,1536]{2,1,0:T(8,128)}, f32[2,3,768,384]{3,2,1,0:T(8,128)}, f32[2,384,768]{2,1,0:T(8,128)}) custom-call(bf16[2,4736,768]{2,1,0:T(8,128)(2,1)} %bitcast.32), custom_call_target="tpu_custom_call" | custom-call | tf_op jit(solution)/shard_map/pallas_call | solution.py:125
  464.3 0.0 copy-done
  464.3 1.1 copy.21
  (2 shorter events, 0.0 us)
Async XLA Ops:
  445.2 19.1 %copy-start = (bf16[2,2,256,768]{3,2,1,0:T(8,128)(2,1)S(1)}, bf16[2,2,256,768]{3,2,1,0:T(8,128)(2,1)}, u32[]{:S(2)}) copy-start(bf16[2,2,256,768]{3,2,1,0:T(8,128)(2,1)} %get-tuple-element.75) | copy-start | bytes 4718596

commit v2 on v1

--- a/solution.py
+++ b/solution.py
@@ -93,52 +93,89 @@
     return jnp.sum(value, axis=0, keepdims=True)
 
 
-def widen_kernel(g_ref, drop, lift, joint, out):
-    number = pl.program_id(1)
-    part = joint.shape[-1]
-    count = pl.num_programs(1)
-
-    @pl.when(number < (count - 2) // 2)
-    def _():
-        drop[...] = wide(g_ref[...])
-
-    @pl.when((number >= (count - 2) // 2) & (number < count - 2))
-    def _():
-        lift[...] = wide(g_ref[...])
-
-    @pl.when(number == count - 2)
-    def _():
-        for i in range(2):
-            joint[0, i] = wide(g_ref[0, :, pl.ds(i * part, part)])
-
-    @pl.when(number == count - 1)
-    def _():
-        for i in range(2):
-            joint[0, 2, pl.ds(i * part, part)] = wide(g_ref[0, pl.ds(0, part), pl.ds(i * part, part)])
-        out[0] = wide(g_ref[0, pl.ds(part, part)])
+def widen_kernel(each, g_ref, drop, lift, joint, out, held, square, triple, last, load_sem, store_sem):
+    streams, _, width = g_ref.shape
+    part = out.shape[1]
+    blocks = 2 * each + 2
+
+    def load(b, i):
+        return pltpu.make_async_copy(
+            g_ref.at[b, pl.ds(i * width, width)], held.at[b, i], load_sem.at[b, i]
+        )
+
+    def store(b, i):
+        if i < each:
+            src, dst = square.at[b, i], drop.at[b, pl.ds(i * width, width)]
+        elif i < 2 * each:
+            src, dst = square.at[b, i], lift.at[b, :, pl.ds((i - each) * width, width)]
+        elif i == 2 * each:
+            src, dst = triple.at[b, pl.ds(0, 2)], joint.at[b, pl.ds(0, 2)]
+        else:
+            src, dst = triple.at[b, 2], joint.at[b, 2]
+        return pltpu.make_async_copy(src, dst, store_sem.at[b, i])
+
+    def store_out(b):
+        return pltpu.make_async_copy(last.at[b], out.at[b], store_sem.at[b, blocks])
+
+    every = [(b, i) for i in range(blocks) for b in range(streams)]
+    for b, i in every:
+        load(b, i).start()
+    size = 64
+    for b, i in every:
+        load(b, i).wait()
+        if i < 2 * each:
+
+            @pl.loop(0, width // size)
+            def _(r):
+                at = pl.ds(pl.multiple_of(r * size, size), size)
+                square[b, i, at] = wide(held[b, i, at])
+
+        elif i == 2 * each:
+
+            @pl.loop(0, width // size)
+            def _(r):
+                at = pl.ds(pl.multiple_of(r * size, size), size)
+                for n in range(2):
+                    triple[b, n, at] = wide(held[b, i, at, pl.ds(n * part, part)])
+
+        else:
+
+            @pl.loop(0, part // size)
+            def _(r):
+                at = pl.ds(pl.multiple_of(r * size, size), size)
+                low_at = pl.ds(pl.multiple_of(part + r * size, size), size)
+                triple[b, 2, at] = wide(held[b, i, at, pl.ds(0, part)])
+                triple[b, 2, low_at] = wide(held[b, i, at, pl.ds(part, part)])
+                last[b, at] = wide(held[b, i, low_at])
+
+            store_out(b).start()
+        store(b, i).start()
+    for b, i in every:
+        store(b, i).wait()
+    for b in range(streams):
+        store_out(b).wait()
 
 
 def widened(grads, inner, part):
     streams, _, width = grads.shape
     each = inner // width
-    block = (1, width, width)
+    f32 = jnp.float32
+    outs = [(streams, inner, width), (streams, width, inner), (streams, 3, width, part), (streams, part, width)]
+    anywhere = pl.BlockSpec(memory_space=pl.ANY)
     return pl.pallas_call(
-        widen_kernel,
-        grid=(streams, 2 * each + 2),
-        in_specs=[pl.BlockSpec(block, lambda b, i: (b, i, 0))],
-        out_specs=[
-            pl.BlockSpec(block, lambda b, i: (b, jnp.minimum(i, each - 1), 0)),
-            pl.BlockSpec(block, lambda b, i: (b, 0, jnp.clip(i - each, 0, each - 1))),
-            pl.BlockSpec((1, 3, width, part), lambda b, i: (b, 0, 0, 0)),
-            pl.BlockSpec((1, part, width), lambda b, i: (b, 0, 0)),
+        partial(widen_kernel, each),
+        in_specs=[anywhere],
+        out_specs=[anywhere] * 4,
+        out_shape=[shape(dims, f32) for dims in outs],
+        scratch_shapes=[
+            pltpu.VMEM((streams, 2 * each + 2, width, width), jnp.bfloat16),
+            pltpu.VMEM((streams, 2 * each, width, width), f32),
+            pltpu.VMEM(outs[2], f32),
+            pltpu.VMEM(outs[3], f32),
+            pltpu.SemaphoreType.DMA((streams, 2 * each + 2)),
+            pltpu.SemaphoreType.DMA((streams, 2 * each + 3)),
         ],
-        out_shape=[
-            shape((streams, inner, width), jnp.float32),
-            shape((streams, width, inner), jnp.float32),
-            shape((streams, 3, width, part), jnp.float32),
-            shape((streams, part, width), jnp.float32),
-        ],
-        compiler_params=pltpu.CompilerParams(vmem_limit_bytes=VMEM_LIMIT),
+        compiler_params=pltpu.CompilerParams(vmem_limit_bytes=52 * 1024 * 1024),
     )(grads)
 
 
@@ -148,9 +185,9 @@
             setattr(self, name, ref)
 
 
-KEPT = ("qkvc", "e", "inv", "normed", "source", "middle", "mixed", "act", "steep", "base")
-WEIGHTS = ("drop", "lift", "joint", "out")
-GIVEN = ("joint", "out", "small", "lift", "drop")
+KEPT = tuple(dict(qkvc=0, e=0, inv=0, normed=0, source=0, middle=0, mixed=0, act=0, steep=0, base=0))
+WEIGHTS = tuple(dict(drop=0, lift=0, joint=0, out=0))
+GIVEN = tuple(dict(joint=0, out=0, small=0, lift=0, drop=0))
 VECTORS = 6
 LOADS = 64
 
@@ -158,18 +195,18 @@
 def kept_shapes(s, packs, every, width, part, inner):
     heads = part // HEAD_DIM
     f32 = jnp.float32
-    dims = {
-        "qkvc": shape((packs, every, 4 * part)),
-        "e": shape((packs, heads, every, every)),
-        "inv": shape((packs, every, part), f32),
-        "normed": shape((packs, every, width)),
-        "source": shape((packs, every, width)),
-        "middle": shape((packs, every, width), f32),
-        "mixed": shape((packs, every, width)),
-        "act": shape((packs, every, inner)),
-        "steep": shape((packs, every, inner)),
-        "base": shape((packs, every, width)),
-    }
+    dims = dict(
+        qkvc=shape((packs, every, 4 * part)),
+        e=shape((packs, heads, every, every)),
+        inv=shape((packs, every, part), f32),
+        normed=shape((packs, every, width)),
+        source=shape((packs, every, width)),
+        middle=shape((packs, every, width), f32),
+        mixed=shape((packs, every, width)),
+        act=shape((packs, every, inner)),
+        steep=shape((packs, every, inner)),
+        base=shape((packs, every, width)),
+    )
     if s == 0:
         dims.pop("source")
     return dims
@@ -177,48 +214,48 @@
 
 def forward_plan(packs, every, width, part, inner):
     full, f32, bf16 = (packs, every, width), jnp.float32, jnp.bfloat16
-    rooms = {
-        "joint": ((2, 3, width, part), bf16),
-        "out": ((2, part, width), bf16),
-        "small_in": ((2, 16, width), bf16),
-        "lift": ((2, width, inner), bf16),
-        "drop": ((2, inner, width), bf16),
-        "dist": ((packs, every, every), f32),
-        "rows_in": (full, bf16),
-        "base": (full, bf16),
-        "dy": (full, bf16),
-        "normed": (full, bf16),
-        "crossed": (full, bf16),
-        "source": (full, bf16),
-        "qkvc": ((packs, every, 4 * part), bf16),
-        "e": ((part // HEAD_DIM, every, every), bf16),
-        "inv": ((packs, every, part), f32),
-        "a_mine": (full, bf16),
-        "a_peer": (full, bf16),
-        "y_mine": (full, bf16),
-        "y_peer": (full, bf16),
-        "middle": (full, f32),
-        "mixed": (full, bf16),
-        "act": ((packs, every, inner), bf16),
-        "steep": ((packs, every, inner), bf16),
-        "scores": ((2, every, every), f32),
-        "hidden": ((2, every, 256), f32),
-    }
+    rooms = dict(
+        joint=((2, 3, width, part), bf16),
+        out=((2, part, width), bf16),
+        small_in=((2, 16, width), bf16),
+        lift=((2, width, inner), bf16),
+        drop=((2, inner, width), bf16),
+        dist=((packs, every, every), f32),
+        rows_in=(full, bf16),
+        base=(full, bf16),
+        dy=(full, bf16),
+        normed=(full, bf16),
+        crossed=(full, bf16),
+        source=(full, bf16),
+        qkvc=((packs, every, 4 * part), bf16),
+        e=((part // HEAD_DIM, every, every), bf16),
+        inv=((packs, every, part), f32),
+        a_mine=(full, bf16),
+        a_peer=(full, bf16),
+        y_mine=(full, bf16),
+        y_peer=(full, bf16),
+        middle=(full, f32),
+        mixed=(full, bf16),
+        act=((packs, every, inner), bf16),
+        steep=((packs, every, inner), bf16),
+        scores=((2, every, every), f32),
+        hidden=((2, every, 256), f32),
+    )
     sem = pltpu.SemaphoreType.DMA
-    flags = {
-        "w_load": sem((5,)),
-        "w_send": sem((5,)),
-        "w_recv": sem((5,)),
-        "d_load": sem((packs,)),
-        "r_load": sem((2, packs)),
-        "r_send": sem((2, 2, 2, packs)),
-        "r_recv": sem((2, 2, packs)),
-        "x_send": sem((2, 2, packs)),
-        "x_recv": sem((2, 2, packs)),
-        "c_send": sem((packs,)),
-        "c_recv": sem((packs,)),
-        "store": sem((LOADS,)),
-    }
+    flags = dict(
+        w_load=sem((5,)),
+        w_send=sem((5,)),
+        w_recv=sem((5,)),
+        d_load=sem((packs,)),
+        r_load=sem((2, packs)),
+        r_send=sem((2, 2, 2, packs)),
+        r_recv=sem((2, 2, packs)),
+        x_send=sem((2, 2, packs)),
+        x_recv=sem((2, 2, packs)),
+        c_send=sem((packs,)),
+        c_recv=sem((packs,)),
+        store=sem((LOADS,)),
+    )
     scratch = [pltpu.VMEM(*spec) for spec in rooms.values()] + list(flags.values())
     return list(rooms) + list(flags), scratch
 
@@ -231,7 +268,8 @@
         del refs[:n]
         return taken
 
-    slopes, rows_ref, dist_ref = take(3)
+    slopes, rows_ref = take(2)
+    dist_refs = take(packs)
     given = dict(zip(GIVEN, take(5)))
     kept = [
         Names(zip([k for k in KEPT if s or k != "source"], take(len(KEPT) - (s == 0)))) for s in range(2)
@@ -267,9 +305,9 @@
         )
 
     def dist_load(m):
-        return pltpu.make_async_copy(dist_ref.at[m], w.dist.at[m], w.d_load.at[m])
-
-    room = ("joint", "out", "small_in", "lift", "drop")
+        return pltpu.make_async_copy(dist_refs[m], w.dist.at[m], w.d_load.at[m])
+
+    room = tuple("small_in" if name == "small" else name for name in GIVEN)
     lands = (w.rows_in, w.dy)
 
     def rows_load(kind, m):
@@ -533,13 +571,13 @@
         pl.pallas_call(
             partial(forward_kernel, packs, names),
             out_shape=outs,
-            in_specs=[pl.BlockSpec(memory_space=pltpu.SMEM)] + [anywhere] * 7,
+            in_specs=[pl.BlockSpec(memory_space=pltpu.SMEM)] + [anywhere] * (6 + packs),
             out_specs=out_specs,
             scratch_shapes=scratch,
             compiler_params=pltpu.CompilerParams(
                 collective_id=1, has_side_effects=True, vmem_limit_bytes=60 * 1024 * 1024
             ),
-        )(slopes, held, distances, *weights)
+        )(slopes, held, *distances, *weights)
     )
     results = []
     for s in range(2):
@@ -882,57 +920,57 @@
 def backward_scratch(packs, rows, width, part, inner, block):
     full, f32 = (packs, 2 * rows, width), jnp.float32
     bf16 = jnp.bfloat16
-    plan = {
-        "drop": ((inner, width), bf16),
-        "lift": ((width, inner), bf16),
-        "joint": ((3, width, part), bf16),
-        "out": ((part, width), bf16),
-        "dy": (full, bf16),
-        "wide_a": ((packs, 2 * rows, inner), bf16),
-        "wide_b": ((packs, 2 * rows, inner), bf16),
-        "narrow": (full, bf16),
-        "source": (full, bf16),
-        "dm_mine": (full, bf16),
-        "dm_peer": (full, bf16),
-        "dn_mine": (full, bf16),
-        "dn_peer": (full, bf16),
-        "crossed": (full, bf16),
-        "middle": (full, f32),
-        "dmid": (full, f32),
-        "da": (full, bf16),
-        "inv": ((packs, 2 * rows, part), f32),
-        "base": (full, bf16),
-        "ends": ((packs, rows, width), f32),
-        "ends_mine": ((packs, rows, width), bf16),
-        "ends_peer": ((packs, rows, width), bf16),
-        "dx": ((packs, rows, width), bf16),
-        "e": ((2, 2, 2 * rows, 2 * rows), bf16),
-        "dc": ((2 * rows, part), f32),
-        "dprob": ((2, 2 * rows, 2 * rows), f32),
-        "ds": ((2, 2 * rows, 2 * rows), bf16),
-        "staged": ((3, 2, 4, block // 8, width), bf16),
-        "sums": ((2, 8, width), f32),
-        "sums_peer": ((2, 8, width), f32),
-        "tail": ((4, block // 8, width), bf16),
-    }
+    plan = dict(
+        drop=((inner, width), bf16),
+        lift=((width, inner), bf16),
+        joint=((3, width, part), bf16),
+        out=((part, width), bf16),
+        dy=(full, bf16),
+        wide_a=((packs, 2 * rows, inner), bf16),
+        wide_b=((packs, 2 * rows, inner), bf16),
+        narrow=(full, bf16),
+        source=(full, bf16),
+        dm_mine=(full, bf16),
+        dm_peer=(full, bf16),
+        dn_mine=(full, bf16),
+        dn_peer=(full, bf16),
+        crossed=(full, bf16),
+        middle=(full, f32),
+        dmid=(full, f32),
+        da=(full, bf16),
+        inv=((packs, 2 * rows, part), f32),
+        base=(full, bf16),
+        ends=((packs, rows, width), f32),
+        ends_mine=((packs, rows, width), bf16),
+        ends_peer=((packs, rows, width), bf16),
+        dx=((packs, rows, width), bf16),
+        e=((2, 2, 2 * rows, 2 * rows), bf16),
+        dc=((2 * rows, part), f32),
+        dprob=((2, 2 * rows, 2 * rows), f32),
+        ds=((2, 2 * rows, 2 * rows), bf16),
+        staged=((3, 2, 4, block // 8, width), bf16),
+        sums=((2, 8, width), f32),
+        sums_peer=((2, 8, width), f32),
+        tail=((4, block // 8, width), bf16),
+    )
     sem = pltpu.SemaphoreType.DMA
-    flags = {
-        "load": sem((LOADS,)),
-        "e_load": sem((2,)),
-        "x_send": sem((2, 2, packs)),
-        "x_recv": sem((2, 2, packs)),
-        "c_send": sem((packs,)),
-        "c_recv": sem((packs,)),
-        "g_store": sem((3,)),
-        "t_store": sem((2,)),
-        "v_send": sem((2,)),
-        "v_recv": sem((2,)),
-        "y_send": sem((packs,)),
-        "y_recv": sem((packs,)),
-        "o_keep": sem((1,)),
-        "o_send": sem((1,)),
-        "o_recv": sem((1,)),
-    }
+    flags = dict(
+        load=sem((LOADS,)),
+        e_load=sem((2,)),
+        x_send=sem((2, 2, packs)),
+        x_recv=sem((2, 2, packs)),
+        c_send=sem((packs,)),
+        c_recv=sem((packs,)),
+        g_store=sem((3,)),
+        t_store=sem((2,)),
+        v_send=sem((2,)),
+        v_recv=sem((2,)),
+        y_send=sem((packs,)),
+        y_recv=sem((packs,)),
+        o_keep=sem((1,)),
+        o_send=sem((1,)),
+        o_recv=sem((1,)),
+    )
     return list(plan) + list(flags), [pltpu.VMEM(*spec) for spec in plan.values()] + list(flags.values())
 
 
@@ -992,7 +1030,8 @@
 
     def ask_rows(s):
         for m in range(packs):
-            ask(("steep", m), kept[s].steep.at[m], w.wide_a.at[m])
+            ask(("act", m), kept[s].act.at[m], w.wide_a.at[m])
+            ask(("steep", m), kept[s].steep.at[m], w.wide_b.at[m])
             ask(("mixed", m), kept[s].mixed.at[m], w.narrow.at[m])
 
     def ask_attention(s):
@@ -1005,8 +1044,8 @@
     for m in range(packs):
         ask(("dy", m), dy_in.at[m], w.dy.at[m])
         ask(("ends", m), y_in.at[m, pl.ds(own, rows)], w.ends_mine.at[m])
+    ask_rows(1)
     ask_layer(1)
-    ask_rows(1)
     ask_attention(1)
 
     clock, ready = [0], [0]
@@ -1087,32 +1126,35 @@
         size = 256
         for number in range(inner // size):
             lanes = pl.ds(number * size, size)
-            grad = dot(w.dy[m], w.drop[lanes], across) * wide(w.wide_a[m, :, lanes])
+            grad = dot(w.dy[m], w.drop[lanes], across) * wide(w.wide_b[m, :, lanes])
             grad = low(grad)
             w.wide_b[m, :, lanes] = grad
             total = column_sum(wide(grad))
             at = number * size
             spot = (s, pl.ds(VECTORS + at // width, 1), pl.ds(at % width, size))
             w.sums[spot] = total if m == 0 else w.sums[spot] + total
-        ask(("act", m), kept[s].act.at[m], w.wide_a.at[m])
         add_sums(s, m, 5, 0.5 * column_sum(wide(w.dy[m])))
         for r in (0, rows):
             at = pl.ds(r, rows)
             w.dm_mine[m, at] = low(dot(w.wide_b[m, at], w.lift[...], across))
         dm[s][m].start()
 
-    def feed_forward_weights(s, spread):
+    def drop_weights(s, spread):
         for m in range(packs):
             got(("act", m))
-            got(("mixed", m))
-        number = 0
-        for first in range(0, inner, block):
+        for number, first in enumerate(range(0, inner, block)):
             lanes = pl.ds(first, block)
             value = product([w.wide_a.at[m, :, lanes] for m in range(packs)], [w.dy.at[m] for m in range(packs)])
             emit(s, number, lambda slot: put(slot, value))
-            number += 1
-            if spread and number % 3 == 0:
+            if number % 3 == 2:
                 ticks(spread)
+        settle_stores()
+        ready[0] = (0 if s else count) + 2 * (inner // block)
+
+    def lift_weights(s, spread):
+        for m in range(packs):
+            got(("mixed", m))
+        number = inner // block
         for column in range(0, inner, width):
             for first in range(0, width, block):
                 value = product(
@@ -1121,7 +1163,7 @@
                 )
                 emit(s, number, lambda slot: put(slot, value))
                 number += 1
-                if spread and number % 3 == 0:
+                if number % 3 == 0:
                     ticks(spread)
         settle_stores()
         ready[0] = (0 if s else count) + 2 * number
@@ -1165,7 +1207,7 @@
                 totals[i] = totals[i] + column_sum(piece)
         for i, row in enumerate((1, 3, 4)):
             add_sums(s, m, row, 0.5 * totals[i])
-        ticks(spread)
+        ticks(1)
         got(("inv", m))
         w.dc[...] = dot(w.da[m], w.out[...], across) * w.inv[m]
         got(("qkvc", m))
@@ -1336,37 +1378,36 @@
         if s:
             for m in range(packs):
                 got(("dy", m))
+            drop_weights(1, 0)
         got("drop")
         got("lift")
         for m in range(packs):
             feed_forward(s, m)
-            if not s:
-                ticks(2)
-        if not s:
+            ticks(1)
+        if s == 0:
             finish_vectors(1)
             for m in range(packs):
                 ends(m)
             pl.when(core == 0)(lambda: edges_hand(w.ends_mine, 0).start())
             pl.when(core == 1)(lambda: edges_keep(w.ends_mine, 1).start())
+            drop_weights(0, 1)
         ask_base(s)
         if s:
             ask_layer(0)
             for m in range(packs):
                 ends_copy(m).start()
-        feed_forward_weights(s, 0 if s else 2)
+        lift_weights(s, 1)
         for m in range(packs):
             attention(s, m, 2, partial(join, m - 1) if s and m else None)
         if s:
             join(packs - 1)
-        if s:
             ask_attention(0)
         attention_weights(s, 1)
         if s:
             ask_rows(0)
         for m in range(packs):
             leave(s, m)
-            if s:
-                ticks(2)
+            ticks(1)
         vectors(s).start()
     finish_vectors(0)
     pl.when(core == 0)(lambda: edges_keep(w.dx, 0).start())
@@ -1434,9 +1475,7 @@
         [norm_gains[0], norm_shifts[0], branch_biases[0], lift_bias[0].reshape(2, -1, width)], axis=1
     )
     small = jnp.concatenate([small, jnp.zeros((2, 16 - small.shape[1], width), small.dtype)], axis=1)
-    distances = jnp.stack(
-        [masked_distance(item_lengths[0, m], key_keep[0, m]) for m in range(packs)]
-    )
+    distances = [masked_distance(item_lengths[0, m], key_keep[0, m]) for m in range(packs)]
     given = (joint_weight[0], output_weight[0], small, lift_weight[0], drop_weight[0])
     kept, weights, small, dy, ends = forward(slopes, held, distances, given)
     line = lax.axis_size("dp") // 2

time: 470 us -> 464 us (0.987)
  Pallas kernels: 452 us -> 447 us
    pallas_call x1, Pallas kernels: 19.1 us -> 14.1 us  [widened(): pl.pallas_call(partial(widen_kernel, each), in_specs=[anywhere], out_spec...]
where the time goes in v2:
time: 464 us; the launch traced here: 461 us
  Pallas kernels  447 us (96%)
  other arithmetic  7.12 us (2%)
  local copies, waits for them, and re-layouts  5.84 us (1%)
    pallas_call x1, Pallas kernels, backward(): pl.pallas_call(partial(backward_kernel, line, count, packs, inside, names...  294 us
    pallas_call x1, Pallas kernels, forward(): pl.pallas_call(partial(forward_kernel, packs, names), out_shape=outs, in_...  139 us
    pallas_call x1, Pallas kernels, widened(): pl.pallas_call(partial(widen_kernel, each), in_specs=[anywhere], out_spec...  14.1 us

profile of v2, /device:TPU:0, one launch (start us, length us, event | category | flops | bytes accessed | tf_op | source)
XLA Modules:
  0.0 460.8 jit_solution(1777525251879545847)
XLA Ops:
  0.6 0.5 multiply_power_fusion.refs_0_
  1.2 0.8 compare_reduce_fusion
  2.0 0.8 slice_bitcast_fusion.6
  2.7 0.2 reduce-window.16
  2.9 0.2 reduce-window.17
  3.1 0.1 convert_reduce_fusion
  3.2 0.1 convert_reduce_fusion.1
  3.2 0.1 select_reduce_fusion.1
  3.3 0.1 fusion.4
  3.5 0.1 fusion.7
  3.6 0.1 fusion.5
  3.7 0.7 reshape_squeeze.3
  4.5 2.0 concatenate.3.refs_6_
  6.4 1.6 sqrt_select_fusion.1.refs_2_
  8.1 1.6 sqrt_select_fusion.refs_3_
  9.7 138.7 %shard_map.178 = (bf16[2,512,1536]{2,1,0:T(8,128)(2,1)}, bf16[2,6,512,512]{3,2,1,0:T(8,128)(2,1)}, f32[2,512,384]{2,1,0:T(8,128)}, bf16[2,512,768]{2,1,0:T(8,128...) custom-call(f32[6]{0:T(128)} %multiply_power_fusion.refs_0_, ...), custom_call_target="tpu_custom_call" | custom-call | tf_op jit(solution)/shard_map/pallas_call | solution.py:571
  148.5 294.0 %shard_map.179 = (bf16[2,2,256,768]{3,2,1,0:T(8,128)(2,1)}, bf16[37,4,32,768]{3,2,1,0:T(8,128)(2,1)}, bf16[37,4,32,768]{3,2,1,0:T(8,128)(2,1)}, bf16[2,37,4,32,768]{4,3,2,1,0:T(8,128)(2,1)}) custom-call(f32[2,16,768]{2,1,0:T(8,128)} %get-tuple-element.45.refs_0_, bf16[2,512,768]{2,1,0:T(8,128)(2,1)} %get-tuple-element.46.refs_1_, ...), custom_call_target="tpu_custom_call" | custom-call | tf_op jit(solution)/shard_map/pallas_call | solution.py:1440
  442.5 0.7 slice_convert_fusion.1
  443.2 0.6 reshape.252
  443.9 0.7 slice_convert_fusion
  444.6 0.6 slice_bitcast_fusion
  445.2 0.0 copy-start
  445.2 14.1 %shard_map.180 = (f32[2,1536,768]{2,1,0:T(8,128)}, f32[2,768,1536]{2,1,0:T(8,128)}, f32[2,3,768,384]{3,2,1,0:T(8,128)}, f32[2,384,768]{2,1,0:T(8,128)}) custom-call(bf16[2,4736,768]{2,1,0:T(8,128)(2,1)} %bitcast.32), custom_call_target="tpu_custom_call" | custom-call | tf_op jit(solution)/shard_map/pallas_call | solution.py:165
  459.4 0.0 copy-done
  459.4 1.1 copy.21
  (2 shorter events, 0.0 us)
Async XLA Ops:
  445.2 14.1 %copy-start = (bf16[2,2,256,768]{3,2,1,0:T(8,128)(2,1)S(1)}, bf16[2,2,256,768]{3,2,1,0:T(8,128)(2,1)}, u32[]{:S(2)}) copy-start(bf16[2,2,256,768]{3,2,1,0:T(8,128)(2,1)} %get-tuple-element.75) | copy-start | bytes 4718596

commit v3 on v2

--- a/solution.py
+++ b/solution.py
@@ -12,8 +12,8 @@
 EPSILON = 1e-06
 SCALE = HEAD_DIM ** (-0.5)
 FAR = 1e30
-CHUNK = 32
-AHEAD = 3
+CHUNK = 48
+AHEAD = 2
 HOP = 2
 VMEM_LIMIT = 44 * 1024 * 1024
 MESH = pl.DeviceIdType.MESH
@@ -93,7 +93,10 @@
     return jnp.sum(value, axis=0, keepdims=True)
 
 
-def widen_kernel(each, g_ref, drop, lift, joint, out, held, square, triple, last, load_sem, store_sem):
+def widen_kernel(
+    each, g_ref, drop, lift, joint, out, gains, shifts, biases, lift_bias,
+    held, square, triple, last, thin, load_sem, thin_sem, store_sem,
+):
     streams, _, width = g_ref.shape
     part = out.shape[1]
     blocks = 2 * each + 2
@@ -117,9 +120,16 @@
     def store_out(b):
         return pltpu.make_async_copy(last.at[b], out.at[b], store_sem.at[b, blocks])
 
+    def load_thin(b):
+        return pltpu.make_async_copy(
+            g_ref.at[b, pl.ds(blocks * width, thin.shape[1])], thin.at[b], thin_sem.at[b]
+        )
+
     every = [(b, i) for i in range(blocks) for b in range(streams)]
     for b, i in every:
         load(b, i).start()
+    for b in range(streams):
+        load_thin(b).start()
     size = 64
     for b, i in every:
         load(b, i).wait()
@@ -150,6 +160,13 @@
 
             store_out(b).start()
         store(b, i).start()
+    for b in range(streams):
+        load_thin(b).wait()
+        rows = wide(thin[b])
+        for i, ref in enumerate((gains, shifts, biases)):
+            ref[b] = rows[2 * i : 2 * i + 2]
+        for i in range(each):
+            lift_bias[b : b + 1, pl.ds(i * width, width)] = rows[VECTORS + i : VECTORS + i + 1]
     for b, i in every:
         store(b, i).wait()
     for b in range(streams):
@@ -161,18 +178,21 @@
     each = inner // width
     f32 = jnp.float32
     outs = [(streams, inner, width), (streams, width, inner), (streams, 3, width, part), (streams, part, width)]
+    outs += [(streams, 2, width)] * 3 + [(streams, inner)]
     anywhere = pl.BlockSpec(memory_space=pl.ANY)
     return pl.pallas_call(
         partial(widen_kernel, each),
         in_specs=[anywhere],
-        out_specs=[anywhere] * 4,
+        out_specs=[anywhere] * 4 + [pl.BlockSpec(memory_space=pltpu.VMEM)] * 4,
         out_shape=[shape(dims, f32) for dims in outs],
         scratch_shapes=[
             pltpu.VMEM((streams, 2 * each + 2, width, width), jnp.bfloat16),
             pltpu.VMEM((streams, 2 * each, width, width), f32),
             pltpu.VMEM(outs[2], f32),
             pltpu.VMEM(outs[3], f32),
+            pltpu.VMEM((streams, 16, width), jnp.bfloat16),
             pltpu.SemaphoreType.DMA((streams, 2 * each + 2)),
+            pltpu.SemaphoreType.DMA((streams,)),
             pltpu.SemaphoreType.DMA((streams, 2 * each + 3)),
         ],
         compiler_params=pltpu.CompilerParams(vmem_limit_bytes=52 * 1024 * 1024),
@@ -938,17 +958,15 @@
         middle=(full, f32),
         dmid=(full, f32),
         da=(full, bf16),
-        inv=((packs, 2 * rows, part), f32),
-        base=(full, bf16),
+        inv=((2 * rows, part), f32),
         ends=((packs, rows, width), f32),
         ends_mine=((packs, rows, width), bf16),
         ends_peer=((packs, rows, width), bf16),
-        dx=((packs, rows, width), bf16),
         e=((2, 2, 2 * rows, 2 * rows), bf16),
         dc=((2 * rows, part), f32),
         dprob=((2, 2 * rows, 2 * rows), f32),
         ds=((2, 2 * rows, 2 * rows), bf16),
-        staged=((3, 2, 4, block // 8, width), bf16),
+        staged=((2, 2, 4, block // 8, width), bf16),
         sums=((2, 8, width), f32),
         sums_peer=((2, 8, width), f32),
         tail=((4, block // 8, width), bf16),
@@ -961,7 +979,7 @@
         x_recv=sem((2, 2, packs)),
         c_send=sem((packs,)),
         c_recv=sem((packs,)),
-        g_store=sem((3,)),
+        g_store=sem((2,)),
         t_store=sem((2,)),
         v_send=sem((2,)),
         v_recv=sem((2,)),
@@ -1039,7 +1057,7 @@
             ask(name, getattr(weights[s], name), getattr(w, name))
         for m in range(packs):
             ask(("middle", m), kept[s].middle.at[m], w.middle.at[m])
-            ask(("inv", m), kept[s].inv.at[m], w.inv.at[m])
+        ask(("inv", 0), kept[s].inv.at[0], w.inv)
 
     for m in range(packs):
         ask(("dy", m), dy_in.at[m], w.dy.at[m])
@@ -1073,11 +1091,11 @@
         at = pl.ds(row, 1)
         w.sums[s, at] = value if m == 0 else w.sums[s, at] + value
 
-    stores = [None, None, None]
+    stores = [None, None]
     stored = [0]
 
     def emit(s, number, fill):
-        slot = stored[0] % 3
+        slot = stored[0] % 2
         stored[0] += 1
         if stores[slot] is not None:
             stores[slot].wait()
@@ -1088,7 +1106,7 @@
         stores[slot].start()
 
     def settle_stores():
-        for slot in range(3):
+        for slot in range(2):
             if stores[slot] is not None:
                 stores[slot].wait()
                 stores[slot] = None
@@ -1146,7 +1164,7 @@
             lanes = pl.ds(first, block)
             value = product([w.wide_a.at[m, :, lanes] for m in range(packs)], [w.dy.at[m] for m in range(packs)])
             emit(s, number, lambda slot: put(slot, value))
-            if number % 3 == 2:
+            if number % 2:
                 ticks(spread)
         settle_stores()
         ready[0] = (0 if s else count) + 2 * (inner // block)
@@ -1163,7 +1181,7 @@
                 )
                 emit(s, number, lambda slot: put(slot, value))
                 number += 1
-                if number % 3 == 0:
+                if number % 2 == 0:
                     ticks(spread)
         settle_stores()
         ready[0] = (0 if s else count) + 2 * number
@@ -1194,7 +1212,12 @@
                 at = pl.ds(r, 32)
                 mine = w.middle[m, pl.ds(pl.multiple_of(own + r, 32), 32)]
                 w.ends[m, at] = mine + wide(w.ends_mine[m, at]) + small[1, pl.ds(5, 1)]
+        if m == 0:
+            ticks(1)
         dm[s][m].wait()
+        if s and m == packs - 1:
+            for n in range(packs):
+                ends_copy(n).start()
         totals = [0.0, 0.0, 0.0]
         for at in row_blocks(every, 32):
             grad = wide(w.dm_mine[m, at]) + wide(w.dm_peer[m, at])
@@ -1209,7 +1232,9 @@
             add_sums(s, m, row, 0.5 * totals[i])
         ticks(1)
         got(("inv", m))
-        w.dc[...] = dot(w.da[m], w.out[...], across) * w.inv[m]
+        w.dc[...] = dot(w.da[m], w.out[...], across) * w.inv[...]
+        if m + 1 < packs:
+            ask(("inv", m + 1), kept[s].inv.at[m + 1], w.inv)
         got(("qkvc", m))
         for pair in range(pairs):
             number = m * pairs + pair
@@ -1290,27 +1315,17 @@
 
             emit(s, number, both)
             number += 1
-            ticks(spread)
-        size = 128
-        per = block // size
-        strips = [("value", r) for r in range(0, part, size)] + [("out", r) for r in range(0, part, size)]
-        for first in range(0, len(strips), per):
-            group = strips[first : first + per]
-
-            def fill(slot):
-                for i, (kind, r) in enumerate(group):
-                    if kind == "value":
-                        for side in range(width // part):
-                            at = pl.ds(side * part + r, size)
-                            value = product([n.at[:, at] for n in source], dv)
-                            put(slot, value, i * size, pl.ds(side * part, part))
-                    else:
-                        value = product([c.at[:, pl.ds(r, size)] for c in context], da)
-                        put(slot, value, i * size)
-
-            emit(s, number, fill)
-            number += 1
-            ticks(spread)
+        ticks(spread)
+
+        def values(slot):
+            for side in range(width // part):
+                at = pl.ds(side * part, part)
+                put(slot, product([n.at[:, at] for n in source], dv), 0, at)
+
+        emit(s, number, values)
+        emit(s, number + 1, lambda slot: put(slot, product(context, da)))
+        number += 2
+        ticks(spread)
         settle_stores()
         ready[0] = (0 if s else count) + 2 * number
 
@@ -1321,12 +1336,12 @@
         for r in range(0, every if s else rows, 32):
             peer, mine = pl.ds(r, 32), pl.ds(r if s else pl.multiple_of(own + r, 32), 32)
             grad = wide(w.dn_mine[m, mine]) + wide(w.dn_peer[m, peer])
-            pulled, along = norm_rows_back(wide(w.base[m, peer]), grad, small[s, pl.ds(0, 1)])
+            pulled, along = norm_rows_back(wide(w.source[m, peer]), grad, small[s, pl.ds(0, 1)])
             result = low(w.dmid[m, mine] + pulled)
             if s:
                 w.dy[m, peer] = result
             else:
-                w.dx[m, peer] = result
+                w.ends_peer[m, peer] = result
             for i, piece in enumerate((along, grad)):
                 totals[i] = totals[i] + column_sum(piece)
         scale = 0.5 if s else 1.0
@@ -1349,7 +1364,7 @@
         w.tail[0] = low(jnp.concatenate([total, pad]))
         tail_store(s).start()
         tail_store(s).wait()
-        ready[0] = count if s else 2 * count
+        ready[0] = max(ready[0], count if s else 2 * count)
 
     def ends_copy(m):
         return remote(
@@ -1370,55 +1385,59 @@
     def ask_base(s):
         for m in range(packs):
             if s:
-                ask(("base", m), kept[s].base.at[m], w.base.at[m])
+                ask(("base", m), kept[s].base.at[m], w.source.at[m])
             else:
-                ask(("base", m), kept[s].base.at[m, pl.ds(own, rows)], w.base.at[m, pl.ds(0, rows)])
-
+                ask(("base", m), kept[s].base.at[m, pl.ds(own, rows)], w.source.at[m, pl.ds(0, rows)])
+
+    for m in range(packs):
+        got(("dy", m))
+    drop_weights(1, 0)
     for s in (1, 0):
-        if s:
-            for m in range(packs):
-                got(("dy", m))
-            drop_weights(1, 0)
-        got("drop")
-        got("lift")
         for m in range(packs):
+            if s == 0:
+                ticks(1)
+                leave(1, m)
+            if m == 0:
+                got("drop")
+                got("lift")
             feed_forward(s, m)
             ticks(1)
         if s == 0:
+            vectors(1).start()
+            drop_weights(0, 1)
             finish_vectors(1)
             for m in range(packs):
                 ends(m)
             pl.when(core == 0)(lambda: edges_hand(w.ends_mine, 0).start())
             pl.when(core == 1)(lambda: edges_keep(w.ends_mine, 1).start())
-            drop_weights(0, 1)
-        ask_base(s)
+            ask_base(0)
         if s:
             ask_layer(0)
-            for m in range(packs):
-                ends_copy(m).start()
         lift_weights(s, 1)
         for m in range(packs):
-            attention(s, m, 2, partial(join, m - 1) if s and m else None)
+            attention(s, m, 1, partial(join, m - 1) if s and m else None)
         if s:
             join(packs - 1)
             ask_attention(0)
         attention_weights(s, 1)
         if s:
+            ask_base(1)
             ask_rows(0)
-        for m in range(packs):
-            leave(s, m)
             ticks(1)
-        vectors(s).start()
+    for m in range(packs):
+        leave(0, m)
+        ticks(1)
+    vectors(0).start()
     finish_vectors(0)
-    pl.when(core == 0)(lambda: edges_keep(w.dx, 0).start())
-    pl.when(core == 1)(lambda: edges_hand(w.dx, 1).start())
+    pl.when(core == 0)(lambda: edges_keep(w.ends_peer, 0).start())
+    pl.when(core == 1)(lambda: edges_hand(w.ends_peer, 1).start())
     if inside:
         run_ticks(clock[0], length)
         drain()
     for m in range(packs):
         dn[0][m].wait_send()
-    edges_keep(w.dx, 0).wait()
-    edges_hand(w.dx, 0).wait()
+    edges_keep(w.ends_peer, 0).wait()
+    edges_hand(w.ends_peer, 0).wait()
 
 
 def backward(line, small, dy, ends, weights, kept, inside):
@@ -1483,10 +1502,7 @@
     edges_out, *grads = backward(line, small, dy, ends, weights, kept, inside)
     grads = grads[2] if inside else reduce_over_dp(grads, line)
     grads = grads.reshape(2, -1, width)
-    weight_rows = 2 * inner + 4 * part
-    drop_grad, lift_grad, joint_grad, output_grad = widened(grads, inner, part)
-    vectors = wide(grads[:, weight_rows : weight_rows + 6])
-    lift_total = wide(grads[:, weight_rows + 6 : weight_rows + 6 + inner // width]).reshape(2, inner)
+    drop_grad, lift_grad, joint_grad, output_grad, *vectors, lift_total = widened(grads, inner, part)
     return (
         edges_out[None],
         joint_grad[None],
@@ -1494,9 +1510,9 @@
         lift_grad[None],
         lift_total[None],
         drop_grad[None],
-        vectors[None, :, 0:2],
-        vectors[None, :, 2:4],
-        vectors[None, :, 4:6],
+        vectors[0][None],
+        vectors[1][None],
+        vectors[2][None],
     )
 
 

time: 464 us -> 485 us (1.045)
  Pallas kernels: 447 us -> 470 us
    pallas_call x1, Pallas kernels: 294 us -> 316 us  [backward(): pl.pallas_call(partial(backward_kernel, line, count, packs, inside, names...]
where the time goes in v3:
time: 485 us; the launch traced here: 481 us
  Pallas kernels  470 us (97%)
  other arithmetic  5.63 us (1%)
    pallas_call x1, Pallas kernels, backward(): pl.pallas_call(partial(backward_kernel, line, count, packs, inside, names...  316 us
    pallas_call x1, Pallas kernels, forward(): pl.pallas_call(partial(forward_kernel, packs, names), out_shape=outs, in_...  139 us
    pallas_call x1, Pallas kernels, widened(): pl.pallas_call(partial(widen_kernel, each), in_specs=[anywhere], out_spec...  14.8 us

profile of v3, /device:TPU:0, one launch (start us, length us, event | category | flops | bytes accessed | tf_op | source)
XLA Modules:
  0.0 481.3 jit_solution(14598383592387385625)
XLA Ops:
  0.6 0.5 multiply_power_fusion.refs_0_
  1.2 0.8 compare_reduce_fusion
  2.0 0.8 slice_bitcast_fusion.3
  2.7 0.2 reduce-window.16
  2.9 0.2 reduce-window.17
  3.1 0.1 convert_reduce_fusion
  3.2 0.1 convert_reduce_fusion.1
  3.2 0.1 select_reduce_fusion.1
  3.3 0.1 fusion.4
  3.5 0.1 fusion.7
  3.6 0.1 fusion.5
  3.7 0.7 reshape_squeeze.3
  4.5 2.0 concatenate.3.refs_6_
  6.4 1.6 sqrt_select_fusion.1.refs_2_
  8.1 1.6 sqrt_select_fusion.refs_3_
  9.7 138.7 %shard_map.178 = (bf16[2,512,1536]{2,1,0:T(8,128)(2,1)}, bf16[2,6,512,512]{3,2,1,0:T(8,128)(2,1)}, f32[2,512,384]{2,1,0:T(8,128)}, bf16[2,512,768]{2,1,0:T(8,128...) custom-call(f32[6]{0:T(128)} %multiply_power_fusion.refs_0_, ...), custom_call_target="tpu_custom_call" | custom-call | tf_op jit(solution)/shard_map/pallas_call | solution.py:591
  148.4 316.5 %shard_map.179 = (bf16[2,2,256,768]{3,2,1,0:T(8,128)(2,1)}, bf16[25,4,48,768]{3,2,1,0:T(8,128)(2,1)}, bf16[25,4,48,768]{3,2,1,0:T(8,128)(2,1)}, bf16[2,25,4,48,768]{4,3,2,1,0:T(8,128)(2,1)}) custom-call(f32[2,16,768]{2,1,0:T(8,128)} %get-tuple-element.49.refs_0_, bf16[2,512,768]{2,1,0:T(8,128)(2,1)} %get-tuple-element.50.refs_1_, ...), custom_call_target="tpu_custom_call" | custom-call | tf_op jit(solution)/shard_map/pallas_call | solution.py:1459
  464.9 0.0 copy-start
  464.9 14.8 %shard_map.180 = (f32[2,1536,768]{2,1,0:T(8,128)}, f32[2,768,1536]{2,1,0:T(8,128)}, f32[2,3,768,384]{3,2,1,0:T(8,128)}, f32[2,384,768]{2,1,0:T(8,128)}, f32[2,2,...) custom-call(bf16[2,4800,768]{2,1,0:T(8,128)(2,1)} %bitcast.28), custom_call_target="tpu_custom_call" | custom-call | tf_op jit(solution)/shard_map/pallas_call | solution.py:183
  479.7 0.0 copy-done
  479.7 1.1 copy.21
  (2 shorter events, 0.0 us)
Async XLA Ops:
  464.9 14.8 %copy-start = (bf16[2,2,256,768]{3,2,1,0:T(8,128)(2,1)S(1)}, bf16[2,2,256,768]{3,2,1,0:T(8,128)(2,1)}, u32[]{:S(2)}) copy-start(bf16[2,2,256,768]{3,2,1,0:T(8,128)(2,1)} %get-tuple-element.79) | copy-start | bytes 4718596
